TPU v7x, 128 devices: a whole 4x4x4 slice. The times are simulated.
128 devices in a mesh: dp: 4 (over x), ctx: 32 (over z, y, core).
Axes of the slice: x: 4, y: 4, z: 4, core: 2. Of those that a mesh axis runs over, the one named last changes fastest.
Arguments:
- queries: bfloat16 [4, 4096, 4096], P('dp', 'ctx'), may hold values from -9.5 to 9.5
- keys: bfloat16 [4, 4096, 512], P('dp', 'ctx'), may hold values from -6 to 6
- values: bfloat16 [4, 4096, 512], P('dp', 'ctx'), may hold values from -6 to 6
- out_grad: bfloat16 [4, 4096, 4096], P('dp', 'ctx'), may hold values from -6 to 6
- segment_ids: int32 [4, 4096], P('dp', 'ctx'), may hold values from 0 to 3, never falling along the last dimension, each value on 1 to 2048 neighbouring positions
- loss_mask: int32 [4, 4096], P('dp', 'ctx'), may hold values from 0 to 1, as said below
Outputs:
- attn_out: bfloat16 [4, 4096, 4096], P('dp', 'ctx')
- q_grad: bfloat16 [4, 4096, 4096], P('dp', 'ctx')
- k_grad: bfloat16 [4, 4096, 512], P('dp', 'ctx')
- v_grad: bfloat16 [4, 4096, 512], P('dp', 'ctx')
Inputs may be any that keep to these rules, and one draw needn't show every extreme that they name: `segment_ids`: document numbers never fall along a sequence; each document holds 1 to 2048 tokens and one holds exactly 2048. `loss_mask`: the last token of every sequence counts.
All inputs are finite; a program needn't handle non-finite values.
Results may differ from a plain program's by a relative error of at most 0.024.
Values may be sent and summed in bfloat16 or wider, within the bound.
No kernel may reach another device: no remote copies, remote signals or barrier semaphores. Data moves between devices by JAX's collectives and lax.ppermute only.
A program may use at most 128 MiB of HBM per device.

v0:
```python
import math

import jax
import jax.numpy as jnp
from jax import lax
from jax.sharding import PartitionSpec as P

QUERY_HEADS = 32
KEY_VALUE_HEADS = 4
HEAD_SIZE = 128


NEG = -1e30


def attend_group(
    query_row_block, gradient_rows, first_row, k_all, v_all, seg_all, key_value_partial
):
    count_of_rows = query_row_block.shape[0]
    sequence_rows = k_all.shape[0]
    rows_per_tile = min(512, sequence_rows)
    grouped_heads = QUERY_HEADS // KEY_VALUE_HEADS
    scale_for_scores = 1.0 / math.sqrt(HEAD_SIZE)
    query_heads = query_row_block.reshape(count_of_rows, KEY_VALUE_HEADS, grouped_heads, HEAD_SIZE)
    gradient_heads = gradient_rows.reshape(count_of_rows, KEY_VALUE_HEADS, grouped_heads, HEAD_SIZE)
    row_pos = first_row + jnp.arange(count_of_rows, dtype=jnp.int32)
    row_seg = lax.dynamic_slice_in_dim(seg_all, first_row, count_of_rows, 0)
    doc_first = jnp.sum((seg_all < row_seg[0]).astype(jnp.int32))
    lower_limit = doc_first // rows_per_tile
    upper_limit = (first_row + count_of_rows - 1) // rows_per_tile + 1

    def scores_at(tile_index):
        tile_start = tile_index * rows_per_tile
        k_tile = lax.dynamic_slice_in_dim(k_all, tile_start, rows_per_tile, 0).reshape(
            rows_per_tile, KEY_VALUE_HEADS, HEAD_SIZE
        )
        v_tile = lax.dynamic_slice_in_dim(v_all, tile_start, rows_per_tile, 0).reshape(
            rows_per_tile, KEY_VALUE_HEADS, HEAD_SIZE
        )
        seg_tile = lax.dynamic_slice_in_dim(seg_all, tile_start, rows_per_tile, 0)
        key_pos = tile_start + jnp.arange(rows_per_tile, dtype=jnp.int32)
        allowed = (key_pos[None, :] <= row_pos[:, None]) & (seg_tile[None, :] == row_seg[:, None])
        scores = (
            jnp.einsum("rgjd,kgd->gjrk", query_heads, k_tile, preferred_element_type=jnp.float32)
            * scale_for_scores
        )
        scores = jnp.where(allowed[None, None], scores, NEG)
        return (scores, k_tile, v_tile, tile_start)

    def max_step(tile_index, carry):
        row_top, row_mass = carry
        scores = scores_at(tile_index)[0]
        new_top = jnp.maximum(row_top, jnp.max(scores, axis=-1))
        row_mass = row_mass * jnp.exp(row_top - new_top) + jnp.sum(
            jnp.exp(scores - new_top[..., None]), axis=-1
        )
        return (new_top, row_mass)

    statistic_shape = (KEY_VALUE_HEADS, grouped_heads, count_of_rows)
    row_top, row_mass = lax.fori_loop(
        lower_limit,
        upper_limit,
        max_step,
        (jnp.full(statistic_shape, NEG, jnp.float32), jnp.zeros(statistic_shape, jnp.float32)),
    )
    log_total = row_top + jnp.log(row_mass)

    def output_update(tile_index, out_total):
        scores, k_tile, v_tile, tile_start = scores_at(tile_index)
        weights = jnp.exp(scores - log_total[..., None]).astype(jnp.bfloat16)
        return out_total + jnp.einsum(
            "gjrk,kgd->rgjd", weights, v_tile, preferred_element_type=jnp.float32
        )

    out_total = lax.fori_loop(
        lower_limit,
        upper_limit,
        output_update,
        jnp.zeros((count_of_rows, KEY_VALUE_HEADS, grouped_heads, HEAD_SIZE), jnp.float32),
    )
    out_heads = out_total.astype(jnp.bfloat16)
    row_delta = jnp.einsum(
        "rgjd,rgjd->gjr", out_heads, gradient_heads, preferred_element_type=jnp.float32
    )

    def grad_step(tile_index, carry):
        dq_total, partial_sum = carry
        scores, k_tile, v_tile, tile_start = scores_at(tile_index)
        probs = jnp.exp(scores - log_total[..., None])
        weights = probs.astype(jnp.bfloat16)
        dweights = jnp.einsum(
            "rgjd,kgd->gjrk", gradient_heads, v_tile, preferred_element_type=jnp.float32
        )
        dscores = (probs * (dweights - row_delta[..., None])).astype(jnp.bfloat16)
        dq_total = dq_total + jnp.einsum(
            "gjrk,kgd->rgjd", dscores, k_tile, preferred_element_type=jnp.float32
        )
        key_gradient_tile = jnp.einsum(
            "gjrk,rgjd->kgd", dscores, query_heads, preferred_element_type=jnp.float32
        )
        value_gradient_tile = jnp.einsum(
            "gjrk,rgjd->kgd", weights, gradient_heads, preferred_element_type=jnp.float32
        )
        stacked_results = jnp.stack([key_gradient_tile, value_gradient_tile]).reshape(
            2, rows_per_tile, KEY_VALUE_HEADS * HEAD_SIZE
        )
        previous = lax.dynamic_slice_in_dim(partial_sum, tile_start, rows_per_tile, 1)
        partial_sum = lax.dynamic_update_slice_in_dim(
            partial_sum, previous + stacked_results, tile_start, 1
        )
        return (dq_total, partial_sum)

    dq_total, key_value_partial = lax.fori_loop(
        lower_limit,
        upper_limit,
        grad_step,
        (
            jnp.zeros((count_of_rows, KEY_VALUE_HEADS, grouped_heads, HEAD_SIZE), jnp.float32),
            key_value_partial,
        ),
    )
    out_rows = out_heads.reshape(count_of_rows, QUERY_HEADS * HEAD_SIZE)
    dq_rows = (
        (dq_total * scale_for_scores)
        .astype(jnp.bfloat16)
        .reshape(count_of_rows, QUERY_HEADS * HEAD_SIZE)
    )
    return (out_rows, dq_rows, key_value_partial)


def body(queries, keys, values, out_grad, segment_ids, loss_mask):
    q_local = queries[0]
    count_of_rows = q_local.shape[0]
    ctx_width = lax.axis_size("ctx")
    ctx_index = lax.axis_index("ctx")
    sequence_rows = count_of_rows * ctx_width
    weight = loss_mask[0].astype(jnp.float32)
    counted = lax.psum(jnp.sum(weight), ("dp", "ctx"))
    scaled = (
        out_grad[0].astype(jnp.float32)
        * weight[:, None]
        * float(lax.axis_size("dp") * sequence_rows)
        / counted
    ).astype(jnp.bfloat16)
    k_all, v_all, seg_all = (
        lax.all_gather(keys[0], "ctx", axis=0, tiled=True),
        lax.all_gather(values[0], "ctx", axis=0, tiled=True),
        lax.all_gather(segment_ids[0].astype(jnp.bfloat16), "ctx", axis=0, tiled=True),
    )
    key_value_partial = jnp.zeros((2, sequence_rows, keys.shape[-1]), jnp.float32)
    out_rows, dq_rows, key_value_partial = attend_group(
        q_local, scaled, ctx_index * count_of_rows, k_all, v_all, seg_all, key_value_partial
    )
    summed = lax.psum_scatter(key_value_partial, "ctx", scatter_dimension=1, tiled=True)
    scale_for_scores = 1.0 / math.sqrt(HEAD_SIZE)
    dk_rows = (summed[0] * scale_for_scores).astype(jnp.bfloat16)
    dv_rows = summed[1].astype(jnp.bfloat16)
    return (out_rows[None], dq_rows[None], dk_rows[None], dv_rows[None])


def solution(mesh):
    in_specs = (
        P("dp", "ctx", None),
        P("dp", "ctx", None),
        P("dp", "ctx", None),
        P("dp", "ctx", None),
        P("dp", "ctx"),
        P("dp", "ctx"),
    )
    out_specs = (
        P("dp", "ctx", None),
        P("dp", "ctx", None),
        P("dp", "ctx", None),
        P("dp", "ctx", None),
    )
    return jax.shard_map(body, mesh=mesh, in_specs=in_specs, out_specs=out_specs, check_vma=False)
```

profile of v0, /device:TPU:1, one launch (start us, length us, event | category | flops | bytes accessed | tf_op | source)
XLA Modules:
  0.0 437.0 jit_solution(8344948127808117049)
XLA Ops:
  7.2 1.7 copy.33
  9.0 1.7 copy.32
  12.7 24.2 %all-gather = bf16[1,4096]{1,0:T(2,128)(2,1)S(1)} all-gather(bf16[1,128]{1,0:T(2,128)(2,1)S(1)} %convert_element_type.51), channel_id=2, replica_groups=mesh['dp'=4,'ctx'=32] {'ctx'}, dimensions={1}, use_global_device_ids=true | all-gather | bytes 8448 | tf_op jit(solution)/shard_map/all_gather | solution.py:148
  37.7 64.5 %psum.7 = f32[]{:T(128)} all-reduce(f32[]{:T(128)} %convert_reduce_fusion.1), channel_id=1, replica_groups=mesh['dp'=4,'ctx'=32] {'dp','ctx'}, use_global_device_ids=true, to_apply=%region_8.9 | all-reduce | flops 1 | bytes 8 | tf_op jit(solution)/shard_map/psum | solution.py:138
  104.8 1.6 copy.34
  107.1 1.7 copy.37
  108.8 1.7 copy.39
  110.4 4.8 %while.37 = (s32[]{:T(128)}, f32[4,8,128]{2,1,0:T(8,128)S(1)}, f32[4,8,128]{2,1,0:T(8,128)S(1)}, s32[]{:T(128)}, bf16[4096]{0:T(1024)(128)(2,1)S(1)}, /*index=5*...) while((s32[]{:T(128)}, f32[4,8,128]{2,1,0:T(8,128)S(1)}, ...), condition=%wide.region_4.5_spmd.clone, body=%wide.region_1.4_spmd.clone.sunk | while | flops 551887488 | bytes 19816892 | solution.py:60
  111.9 1.5 fusion.75
  113.4 1.8 exponential_reduce_fusion.2
  116.1 1.6 broadcast.154.clone
  117.7 8.4 %while.38 = (s32[]{:T(128)}, f32[128,4,8,128]{0,3,2,1:T(8,128)}, s32[]{:T(128)}, bf16[4096,512]{0,1:T(8,128)(2,1)}, bf16[4096]{0:T(1024)(128)(2,1)S(1)}, /*index...) while((s32[]{:T(128)}, f32[128,4,8,128]{0,3,2,1:T(8,128)}, ...), condition=%wide.region_6.7_spmd.clone, body=%wide.region_5.6_spmd.clone.sunk | while | flops 1082983040 | bytes 8544707 | solution.py:75
  119.2 6.9 %bitcast_add_fusion.4 = f32[128,4,8,128]{0,3,2,1:T(8,128)} fusion(f32[128,4,8,128]{0,3,2,1:T(8,128)} %get-tuple-element.631, bf16[512,4,128,1]{0,2,3,1:T(8,128)(2,1)S(1)} %bitcast.172, f32[4,8,128]{2,1,0:T(8,128)S(1)} %get-tuple-element.652, pred[128,512]{1,0:T(8,128)(4,1)S(1)} %compare_and_fusion.7, bf16[512,4,128,1]{0,2,3,1:T(8,128)(2,1)S(1)} %bitcast.171, ...), kind=kOutput, calls=%fused_computation.21.clone.1 | convolution fusion | flops 1082654720 | bytes 6373376 | tf_op jit(solution)/shard_map/while/body/gjrk,kgd->rgjd/dot_general | solution.py:71
  126.1 4.8 %fusion.34 = (f32[4,8,128]{2,1,0:T(8,128)S(1)}, bf16[128,4,8,128]{0,3,2,1:T(8,128)(2,1)}, bf16[128,4,8,128]{0,3,2,1:T(8,128)(2,1)}) fusion(f32[]{:T(128)} %psum.7, f32[128,4,8,128]{0,3,2,1:T(8,128)} %bitcast.173, f32[128]{0:T(128)S(1)} %convert_bitcast_fusion, f32[128,4,8,128]{0,3,2,1:T(8,128)} %get-tuple-element.177), kind=kLoop, calls=%fused_computation.51 | loop fusion | flops 4714496 | bytes 6308356 | tf_op jit(solution)/shard_map/rgjd,rgjd->gjr/dot_general | solution.py:82
  130.8 1.6 broadcast.154
  132.4 7.9 %broadcast_in_dim.61.clone = f32[2,4096,512]{2,1,0:T(8,128)} broadcast(f32[]{:T(128)} %constant.83.clone.1), dimensions={} | broadcast | bytes 16777220 | tf_op jit(solution)/shard_map/broadcast_in_dim | solution.py:150
  140.3 24.9 %while.39 = (s32[]{:T(128)}, f32[128,4,8,128]{0,3,2,1:T(8,128)}, f32[2,4096,512]{2,1,0:T(8,128)}, s32[]{:T(128)}, bf16[4096,512]{0,1:T(8,128)(2,1)}, /*index=5*/...) while((s32[]{:T(128)}, f32[128,4,8,128]{0,3,2,1:T(8,128)}, ...), condition=%wide.region_10.11_spmd.clone, body=%wide.region_9.10_spmd.clone.sunk | while | flops 2707227136 | bytes 100393584 | solution.py:113
  140.6 2.3 constant_dynamic-slice_fusion.13
  142.9 3.1 constant_dynamic-slice_fusion.14
  146.0 1.9 copy.85
  147.9 2.4 fusion.90
  150.4 2.2 fusion.92
  152.5 3.0 fusion.91
  155.5 1.5 fusion.93
  157.3 1.3 bitcast_add_fusion.5
  158.6 1.4 copy-done.2
  160.0 1.8 maximum_add_fusion.2
  161.8 1.9 copy.86
  163.7 1.5 constant_dynamic-update-slice_fusion.2
  169.4 257.9 %reduce-scatter.2.cloned.1.call-done = f32[2,128,512]{2,1,0:T(8,128)} async-done(((f32[2,4096,512]{2,1,0:T(8,128)}), f32[2,128,512]{2,1,0:T(8,128)}) %reduce-scatter.2.cloned.1.call-update) | async-done | bytes 524304 | tf_op jit(solution)/shard_map/reduce_scatter | solution.py:154
  427.3 1.6 slice.20
  428.9 1.6 fusion.35
  (58 shorter events, 12.0 us)
Async XLA Ops:
  7.2 101.6 %copy-start.6 = (bf16[1,128,4096]{2,1,0:T(8,128)(2,1)S(1)}, bf16[1,128,4096]{2,1,0:T(8,128)(2,1)}, u32[]{:S(2)}) copy-start(bf16[1,128,4096]{2,1,0:T(8,128)(2,1)} %param.15) | copy-start | bytes 3145732
  7.2 103.2 %all-gather.8.cloned.1.call-start = ((), (), s32[]{:S(2)}) async-start(), calls=%async_computation.3 | async-start | bytes 4325376 | tf_op jit(solution)/shard_map/all_gather | solution.py:146
  9.0 107.1 %all-gather.6.cloned.1.call-start = ((), (), s32[]{:S(2)}) async-start(), calls=%async_computation.2 | async-start | bytes 4325376 | tf_op jit(solution)/shard_map/all_gather | solution.py:147
  10.7 416.5 %reduce-scatter.2.cloned.1.call-start = ((), (), s32[]{:S(2)}) async-start(), calls=%async_computation.1 | async-start | bytes 17301504 | tf_op jit(solution)/shard_map/reduce_scatter | solution.py:154
  106.4 4.0 copy-start.9
  110.4 7.2 %copy-start.7 = (bf16[128,4,8,128]{3,2,1,0:T(8,128)(2,1)S(1)}, bf16[128,4,8,128]{3,2,1,0:T(8,128)(2,1)}, u32[]{:S(2)}) copy-start(bf16[128,4,8,128]{3,2,1,0:T(8,128)(2,1)} %copy.37) | copy-start | bytes 3145732
  147.9 2.4 copy-start.8
  150.4 2.2 copy-start.4
  155.5 1.5 copy-start
  155.5 1.8 copy-start.1
  158.6 1.4 copy-start.2
  165.2 1.2 copy-start.5
  165.2 2.5 copy-start.3
Sparse Core Ops, SparseCore 0:
  10.8 53.4 all-gather.7
  67.0 49.0 all-gather.5
  165.4 261.8 reduce-scatter.1
where the time goes:
time: 439 us; the launch traced here: 437 us
  waiting for transfers between devices  259 us (59%)
  blocking collectives  88.7 us (20%)
  local copies, waits for them, and re-layouts  40.5 us (9%)
  matrix products  18.7 us (4%)
  between operations  16.5 us (4%)
  other arithmetic  13.5 us (3%)
    reduce_scatter x1, waiting for transfers between devices, body(): lax.psum_scatter(key_value_partial, 'ctx', scatter_dimension=1, tiled=True)  258 us
    psum x1, blocking collectives, body(): counted = lax.psum(jnp.sum(weight), ('dp', 'ctx'))  64.5 us
    all_gather x1, blocking collectives, body(): lax.all_gather(segment_ids[0].astype(jnp.bfloat16), 'ctx', axis=0, tiled=...  24.2 us
  transfers between devices with their start and end apart: 3, of which 2 were waited for; matrix products, arithmetic and copies ran while one was open for 4% of the time, Pallas kernels for 0%

commit v1 on v0

v1 whole, which is shorter than its diff:
```python
import math, functools
import jax, jax.numpy as jnp
from jax import lax
from jax.sharding import PartitionSpec as P
from jax.experimental import pallas as pl
from jax.experimental.pallas import tpu as pltpu

NEG = -1e30
CH = math.log2(math.e) / math.sqrt(128)
BF, F32 = jnp.bfloat16, jnp.float32
NB = 9
NT = (((1,), (1,)), ((), ()))


def mm(a, b):
    return jnp.dot(a, b, preferred_element_type=F32)


def mmt(a, b):
    return lax.dot_general(a, b, NT, preferred_element_type=F32)


def attend_kernel(s_ref, qo_ref, qs_ref, go_ref, gs_ref, own_ref, za_ref, zc_ref, y1_ref, y2_ref, y3_ref,
                  oo_ref, os_ref, dqo_ref, dqs_ref, p1_ref, p2_ref, p3_ref, loc_ref,
                  kk, vv, kt, vt, bias, sc, pp, ds, dka, dva):
    core, z, y = s_ref[0], s_ref[1], s_ref[2]
    chip = 4 * z + y
    blocks = [(own_ref, (), None), (za_ref, (), chip - 4), (zc_ref, (), chip - 8)]
    for s, r in ((1, y1_ref), (2, y2_ref), (3, y3_ref)):
        turned = lax.rem(y - s + 4, 4)
        blocks.append((r, (0,), 4 * z - 4 + turned))
        blocks.append((r, (1,), chip - s - jnp.where(y >= s, 0, 4)))
    lane = lax.broadcasted_iota(jnp.int32, (1, 128), 1)
    t_seg = jnp.concatenate([own_ref[0, 256:257], own_ref[1, 256:257]], axis=1).astype(F32)
    t_mask = jnp.concatenate([own_ref[0, 257:258], own_ref[1, 257:258]], axis=1).astype(F32)
    t_pos = jnp.concatenate([core * 128 + lane, (1 - core) * 128 + lane], axis=1)
    key = lax.broadcasted_iota(jnp.int32, (128, 256), 0)
    for b, (ref, pre, idx) in enumerate(blocks):
        for o in range(2):
            r0 = b * 256 + o * 128
            k = ref[pre + (o, slice(0, 128))]
            v = ref[pre + (o, slice(128, 256))]
            kk[r0:r0 + 128] = k
            vv[r0:r0 + 128] = v
            kt[:, r0:r0 + 128] = k.T
            vt[:, r0:r0 + 128] = v.T
            k_seg = ref[pre + (o, slice(256, 257))].astype(F32)
            n = [jnp.sum((k_seg < s).astype(F32), axis=1, keepdims=True) for s in (1, 2, 3)]
            first = jnp.where(t_seg == 3, n[2], jnp.where(t_seg == 2, n[1], jnp.where(t_seg == 1, n[0], 0.0)))
            first = first.astype(jnp.int32)
            if idx is None:
                at = core * 128 if o == 0 else (1 - core) * 128
                ok = (key >= first) & (key + at <= t_pos)
            else:
                first = jnp.where(idx >= 0, first, 128)
                ok = key >= first
            bias[r0:r0 + 128] = jnp.where(ok, 0.0, NEG)
    dka[...] = jnp.zeros_like(dka)
    dva[...] = jnp.zeros_like(dva)

    def head(h, _):
        cols = pl.ds(pl.multiple_of(h * 128, 128), 128)
        q = jnp.concatenate([qo_ref[:, cols], qs_ref[:, cols]], axis=0)
        g = jnp.concatenate([go_ref[:, cols], gs_ref[:, cols]], axis=0)
        top = jnp.full((8, 256), NEG, F32)
        for b in range(NB):
            rows = slice(b * 256, b * 256 + 256)
            s = mmt(kk[rows], q) + bias[rows]
            sc[rows] = s
            top = jnp.maximum(top, jnp.max(s.reshape(32, 8, 256), axis=0))
        top = jnp.max(top, axis=0, keepdims=True) * CH
        mass = jnp.zeros((8, 256), F32)
        for b in range(NB):
            rows = slice(b * 256, b * 256 + 256)
            p = jnp.exp2(sc[rows] * CH - top)
            mass = mass + jnp.sum(p.reshape(32, 8, 256), axis=0)
            pp[rows] = p.astype(BF)
        inv = 1.0 / jnp.sum(mass, axis=0, keepdims=True)
        ot = (mm(vt[...], pp[...]) * inv).astype(BF)
        out = ot.T
        oo_ref[:, cols] = out[:128]
        os_ref[:, cols] = out[128:]
        delta = jnp.sum(ot.astype(F32) * g.T.astype(F32), axis=0, keepdims=True)
        inv = inv * t_mask
        col = jnp.broadcast_to(inv, (128, 256)).T
        qn = (q.astype(F32) * col).astype(BF)
        gn = (g.astype(F32) * col).astype(BF)
        for b in range(NB):
            rows = slice(b * 256, b * 256 + 256)
            p = pp[rows]
            d = (p.astype(F32) * (mmt(vv[rows], g) - delta)).astype(BF)
            ds[rows] = d
            dva[rows] += mm(p, gn)
            dka[rows] += mm(d, qn)
        dq = (mm(kt[...], ds[...]) * (inv * (1.0 / math.sqrt(128)))).astype(BF).T
        dqo_ref[:, cols] = dq[:128]
        dqs_ref[:, cols] = dq[128:]
        return 0

    lax.fori_loop(0, 8, head, 0)
    for b in range(NB):
        for o in range(2):
            rows = slice(b * 256 + o * 128, b * 256 + o * 128 + 128)
            if b < 3:
                loc_ref[b, o, 0] = dka[rows]
                loc_ref[b, o, 1] = dva[rows]
            else:
                ref = (p1_ref, p2_ref, p3_ref)[(b - 3) // 2]
                ref[(b - 3) % 2, o, 0] = dka[rows].astype(BF)
                ref[(b - 3) % 2, o, 1] = dva[rows].astype(BF)


def attend(scal, j, q, qs, g, gs, own, za, zc, y1, y2, y3):
    wide = lambda f: pl.BlockSpec((128, 1024), f)
    whole = lambda a: pl.BlockSpec(a.shape, lambda i, s, n=a.ndim: (0,) * n)
    mine = wide(lambda i, s: (0, s[0] * 2 + j))
    other = wide(lambda i, s: (0, j))
    rows = jax.ShapeDtypeStruct((128, 1024), BF)
    part = jax.ShapeDtypeStruct((2, 2, 2, 128, 128), BF)
    loc = jax.ShapeDtypeStruct((3, 2, 2, 128, 128), F32)
    outs = [rows] * 4 + [part] * 3 + [loc]
    n = NB * 256
    return pl.pallas_call(
        attend_kernel,
        out_shape=outs,
        grid_spec=pltpu.PrefetchScalarGridSpec(
            num_scalar_prefetch=1,
            grid=(1,),
            in_specs=[mine, other, mine, other] + [whole(a) for a in (own, za, zc, y1, y2, y3)],
            out_specs=[whole(o) for o in outs],
            scratch_shapes=[
                pltpu.VMEM((n, 128), BF), pltpu.VMEM((n, 128), BF), pltpu.VMEM((128, n), BF), pltpu.VMEM((128, n), BF),
                pltpu.VMEM((n, 256), F32), pltpu.VMEM((n, 256), F32), pltpu.VMEM((n, 256), BF), pltpu.VMEM((n, 256), BF),
                pltpu.VMEM((n, 128), F32), pltpu.VMEM((n, 128), F32),
            ],
        ),
        compiler_params=pltpu.CompilerParams(vmem_limit_bytes=48 * 2**20),
        name="attend",
    )(scal, q, qs, g, gs, own, za, zc, y1, y2, y3)


def shard(queries, keys, values, out_grad, segment_ids, loss_mask):
    me = lax.axis_index("ctx")
    core, y, z = me % 2, me // 2 % 4, me // 8
    q, k, v, g = queries[0], keys[0], values[0], out_grad[0]

    def send(x, target):
        pairs = []
        for i in range(32):
            zz, yy, cc = target(i // 8, i // 2 % 4, i % 2)
            if 0 <= zz < 4:
                pairs.append((i, (zz * 4 + yy % 4) * 2 + cc % 2))
        return lax.ppermute(x, "ctx", pairs)

    swap = lambda x: send(x, lambda z, y, c: (z, y, c + 1))
    along_z = lambda x, a: send(x, lambda z, y, c: (z + a, y, c))
    along_y = lambda x, s: send(x, lambda z, y, c: (z, y + s, c))

    counted = jnp.sum(loss_mask.astype(F32), axis=1, keepdims=True)
    counted = counted + swap(counted)
    for step in (1, 2):
        counted = counted + lax.ppermute(counted, "dp", [(i, i ^ step) for i in range(4)])
        counted = counted + send(counted, lambda z, y, c: (z, y ^ step, c))
        counted = counted + send(counted, lambda z, y, c: (z ^ step, y, c))

    info = jnp.concatenate([segment_ids.astype(BF), loss_mask.astype(BF), jnp.zeros((14, 128), BF)], axis=0)

    def payload(c):
        heads = lambda a: lax.dynamic_slice(a, (0, c * 256), (128, 256)).reshape(128, 2, 128).transpose(1, 0, 2)
        return jnp.concatenate([heads(k), heads(v), jnp.broadcast_to(info, (2, 16, 128))], axis=1)

    own = jnp.stack([payload(core), swap(payload(1 - core))], axis=1)
    half = lambda a, c: lax.dynamic_slice(a, (0, c * 2048), (128, 2048))
    za, zc = along_z(own, 1), along_z(own, 2)
    qs, gs = swap(half(q, 1 - core)), swap(half(g, 1 - core))
    scal = jnp.stack([core, z, y]).astype(jnp.int32)

    ys = []
    for j in range(2):
        ys.append([
            along_y(jnp.stack([za[j], jnp.where(y + s < 4, own[j], zc[j])]), s) for s in (1, 2, 3)
        ])
    rows_out, grads = [], []
    for j in range(2):
        oo, os, dqo, dqs, p1, p2, p3, loc = attend(scal, j, q, qs, g, gs, own[j], za[j], zc[j], *ys[j])
        rows_out.append((oo, dqo, swap(jnp.stack([os, dqs]))))
        got = [along_y(p, -s) for s, p in ((1, p1), (2, p2), (3, p3))]
        got = [a.astype(F32) for a in got]
        back_a, back_c, here = loc[1], loc[2], loc[0]
        for s in (1, 2, 3):
            a = got[s - 1]
            back_a = back_a + a[0]
            here = here + jnp.where(y + s < 4, a[1], 0.0)
            back_c = back_c + jnp.where(y + s < 4, 0.0, a[1])
        grads.append(here + along_z(back_a.astype(BF), -1).astype(F32) + along_z(back_c.astype(BF), -2).astype(F32))
    scale = float(lax.axis_size("dp") * 4096) / counted[0, 0]
    total = jnp.stack(grads) * (jnp.array([1.0 / math.sqrt(128), 1.0], F32)[None, None, :, None, None] * scale)
    total = total.astype(BF)
    mine, theirs = total[:, 0], swap(total[:, 1])

    def join(a, b, axis):
        return jnp.concatenate([jnp.where(core == 0, a, b), jnp.where(core == 0, b, a)], axis=axis)

    both = join(mine, theirs, 0).transpose(1, 2, 0, 3).reshape(2, 128, 512)
    attn = join(jnp.concatenate([r[0] for r in rows_out], 1), jnp.concatenate([r[2][0] for r in rows_out], 1), 1)
    dq = join(jnp.concatenate([r[1] for r in rows_out], 1), jnp.concatenate([r[2][1] for r in rows_out], 1), 1)
    dq = (dq.astype(F32) * scale).astype(BF)
    return attn[None], dq[None], both[0][None], both[1][None]


def solution(mesh):
    rows, ids = P("dp", "ctx", None), P("dp", "ctx")
    return jax.shard_map(
        shard, mesh=mesh, in_specs=(rows,) * 4 + (ids,) * 2, out_specs=(rows,) * 4, check_vma=False
    )
```

time: 439 us -> 166 us (0.38)
  waiting for transfers between devices: 259 us -> 21.9 us
  blocking collectives: 88.7 us -> 0 us
  starting transfers between devices: 0.12 us -> 68.6 us
  Pallas kernels: 0 us -> 53.7 us
  local copies, waits for them, and re-layouts: 40.5 us -> 6.41 us
  matrix products: 18.7 us -> 0 us
  between operations: 16.5 us -> 6.22 us
  other arithmetic: 13.5 us -> 8.88 us
    reduce_scatter x1 -> x0, waiting for transfers between devices: 258 us -> none  [body(): lax.psum_scatter(key_value_partial, 'ctx', scatter_dimension=1, tiled=True)]
    ppermute x0 -> x31, starting transfers between devices: none -> 68.6 us  [the longest x29 63 us: send(): return lax.ppermute(x, 'ctx', pairs)]
    psum x1 -> x0, blocking collectives: 64.5 us -> none  [body(): counted = lax.psum(jnp.sum(weight), ('dp', 'ctx'))]
    pallas_call x0 -> x2, Pallas kernels: none -> 53.7 us  [attend(): pl.pallas_call(attend_kernel, out_shape=outs, grid_spec=pltpu.PrefetchSca...]
    all_gather x1 -> x0, blocking collectives: 24.2 us -> none  [body(): lax.all_gather(segment_ids[0].astype(jnp.bfloat16), 'ctx', axis=0, tiled=...]
    ppermute x0 -> x31, waiting for transfers between devices: none -> 21.9 us  [the longest x29 20.7 us: send(): return lax.ppermute(x, 'ctx', pairs)]
    dot_general x7 -> x0, matrix products: 18.7 us -> none  [the longest x1 6.89 us: output_update(): jnp.einsum('gjrk,kgd->rgjd', weights, v_tile, preferred_element_type=jnp....]
    broadcast_in_dim x3 -> x2, local copies, waits for them, and re-layouts: 7.89 us -> 0.01 us  [the longest x1 0.01 us: payload(): jnp.broadcast_to(info, (2, 16, 128))]
  transfers between devices with their start and end apart: 3 -> 31, of which waited for: 2 -> 15; matrix products, arithmetic and copies ran while one was open for 4% -> 6% of each run, Pallas kernels for 0% -> 32%
where the time goes in v1:
time: 166 us
  starting transfers between devices  68.6 us (41%)
  Pallas kernels  53.7 us (32%)
  waiting for transfers between devices  21.9 us (13%)
  other arithmetic  8.88 us (5%)
  local copies, waits for them, and re-layouts  6.41 us (4%)
  between operations  6.22 us (4%)
    ppermute x29, starting transfers between devices, send(): return lax.ppermute(x, 'ctx', pairs)  63 us
    pallas_call x2, Pallas kernels, attend(): pl.pallas_call(attend_kernel, out_shape=outs, grid_spec=pltpu.PrefetchSca...  53.7 us
    ppermute x29, waiting for transfers between devices, send(): return lax.ppermute(x, 'ctx', pairs)  20.7 us
    ppermute x2, starting transfers between devices, shard(): lax.ppermute(counted, 'dp', [(i, i ^ step) for i in range(4)])  5.56 us
  transfers between devices with their start and end apart: 31, of which 15 were waited for; matrix products, arithmetic and copies ran while one was open for 6% of the time, Pallas kernels for 32%

profile of v1, /device:TPU:1, one launch (start us, length us, event | category | flops | bytes accessed | tf_op | source)
XLA Modules:
  0.0 165.6 jit_solution(5971318789889977605)
XLA Ops:
  2.9 1.5 collective-permute-start.2
  6.1 5.6 %collective-permute-start.4 = (bf16[2,2,272,128]{3,2,1,0:T(8,128)(2,1)}, bf16[2,2,272,128]{3,2,1,0:T(8,128)(2,1)S(1)}, u32[]{:S(2)}, u32[]{:S(2)}) collective-permute-start(bf16[2,2,272,128]{3,2,1,0:T(8,128)(2,1)} %pad_maximum_fusion.4), channel_id=1, source_target_pairs={{0,16},{1,17},{2,18},{3,19},{4,20},{5,21},{6,22},{7,23},{8,24},{9,... | collective-permute-start | bytes 835592 | tf_op jit(solution)/shard_map/ppermute | solution.py:153
  14.0 2.6 %collective-permute-start.3 = (bf16[2,2,272,128]{3,2,1,0:T(8,128)(2,1)}, bf16[2,2,272,128]{3,2,1,0:T(8,128)(2,1)S(1)}, u32[]{:S(2)}, u32[]{:S(2)}) collective-permute-start(bf16[2,2,272,128]{3,2,1,0:T(8,128)(2,1)} %pad_maximum_fusion.4), channel_id=1, source_target_pairs={{0,8},{1,9},{2,10},{3,11},{4,12},{5,13},{6,14},{7,15},{8,16},{9,17... | collective-permute-start | bytes 835592 | tf_op jit(solution)/shard_map/ppermute | solution.py:153
  18.4 5.2 %collective-permute-done.3 = bf16[2,2,272,128]{3,2,1,0:T(8,128)(2,1)S(1)} collective-permute-done((bf16[2,2,272,128]{3,2,1,0:T(8,128)(2,1)}, bf16[2,2,272,128]{3,2,1,0:T(8,128)(2,1)S(1)}, u32[]{:S(2)}, u32[]{:S(2)}) %collective-permute-start.3) | collective-permute-done | bytes 278560 | tf_op jit(solution)/shard_map/ppermute | solution.py:153
  25.3 1.3 collective-permute-start.5
  27.3 1.5 collective-permute-start.13
  28.7 1.2 collective-permute-done.13
  31.1 2.0 %collective-permute-start.14 = (f32[1,1]{1,0:T(1,128)}, f32[1,1]{1,0:T(1,128)}, u32[]{:S(2)}, u32[]{:S(2)}) collective-permute-start(f32[1,1]{1,0:T(1,128)} %add.166), channel_id=1, source_target_pairs={{0,32},{32,0},{64,96},{96,64},{1,33},{33,1},{65,97},{97,65},{2,34}... | collective-permute-start | bytes 20 | tf_op jit(solution)/shard_map/ppermute | solution.py:162
  34.5 2.1 %collective-permute-start.15 = (f32[1,1]{1,0:T(1,128)}, f32[1,1]{1,0:T(1,128)}, u32[]{:S(2)}, u32[]{:S(2)}) collective-permute-start(f32[1,1]{1,0:T(1,128)} %add.167), channel_id=1, source_target_pairs={{0,2},{1,3},{2,0},{3,1},{4,6},{5,7},{6,4},{7,5},{8,10},{9,11},{10,... | collective-permute-start | bytes 20 | tf_op jit(solution)/shard_map/ppermute | solution.py:153
  37.6 2.9 %collective-permute-start.16 = (f32[1,1]{1,0:T(1,128)}, f32[1,1]{1,0:T(1,128)}, u32[]{:S(2)}, u32[]{:S(2)}) collective-permute-start(f32[1,1]{1,0:T(1,128)} %add.168), channel_id=1, source_target_pairs={{0,8},{1,9},{2,10},{3,11},{4,12},{5,13},{6,14},{7,15},{8,0},{9,1},... | collective-permute-start | bytes 20 | tf_op jit(solution)/shard_map/ppermute | solution.py:153
  41.3 3.5 %collective-permute-start.17 = (f32[1,1]{1,0:T(1,128)}, f32[1,1]{1,0:T(1,128)}, u32[]{:S(2)}, u32[]{:S(2)}) collective-permute-start(f32[1,1]{1,0:T(1,128)} %add.169), channel_id=1, source_target_pairs={{0,64},{32,96},{64,0},{96,32},{1,65},{33,97},{65,1},{97,33},{2,66}... | collective-permute-start | bytes 20 | tf_op jit(solution)/shard_map/ppermute | solution.py:162
  45.8 3.4 %collective-permute-start.18 = (f32[1,1]{1,0:T(1,128)}, f32[1,1]{1,0:T(1,128)}, u32[]{:S(2)}, u32[]{:S(2)}) collective-permute-start(f32[1,1]{1,0:T(1,128)} %add.170), channel_id=1, source_target_pairs={{0,4},{1,5},{2,6},{3,7},{4,0},{5,1},{6,2},{7,3},{8,12},{9,13},{10,... | collective-permute-start | bytes 20 | tf_op jit(solution)/shard_map/ppermute | solution.py:153
  50.4 3.8 %collective-permute-start.19 = (f32[1,1]{1,0:T(1,128)}, f32[1,1]{1,0:T(1,128)}, u32[]{:S(2)}, u32[]{:S(2)}) collective-permute-start(f32[1,1]{1,0:T(1,128)} %add.171), channel_id=1, source_target_pairs={{0,16},{1,17},{2,18},{3,19},{4,20},{5,21},{6,22},{7,23},{8,24},{9,... | collective-permute-start | bytes 20 | tf_op jit(solution)/shard_map/ppermute | solution.py:153
  54.2 2.6 %collective-permute-start.6 = (bf16[2,2,272,128]{3,2,1,0:T(8,128)(2,1)}, bf16[2,2,272,128]{3,2,1,0:T(8,128)(2,1)}, u32[]{:S(2)}, u32[]{:S(2)}) collective-permute-start(bf16[2,2,272,128]{3,2,1,0:T(8,128)(2,1)} %get-tuple-element.79), channel_id=1, source_target_pairs={{0,4},{1,5},{2,6},{3,7},{4,0},{5,1},{6,2},{7,3},{8,12},{9,13},{10,... | collective-permute-start | bytes 835592 | tf_op jit(solution)/shard_map/ppermute | solution.py:153
  56.8 1.9 %pad_maximum_fusion.8 = (bf16[2,2,272,128]{3,2,1,0:T(8,128)(2,1)}, bf16[2,2,272,128]{3,2,1,0:T(8,128)(2,1)}, bf16[2,2,272,128]{3,2,1,0:T(8,128)(2,1)}) fusion(bf16[1,2,272,128]{3,2,1,0:T(8,128)(2,1)} %get-tuple-element.68, bf16[1,2,272,128]{3,2,1,0:T(8,128)(2,1)} %get-tuple-element.40, bf16[1,2,272,128]{3,2,1,0:T(8,128)(2,1)S(1)} %get-tuple-element.59, ...), kind=kLoop, calls=%fused_computation.22 | loop fusion | flops 417792 | bytes 1392640 | tf_op jit(solution)/shard_map/stack | solution.py:181
  58.7 1.1 collective-permute-start.7
  59.9 1.4 collective-permute-start.8
  62.8 1.6 collective-permute-done.7.y3_ref
  64.4 26.8 %attend.2 = (bf16[128,1024]{1,0:T(8,128)(2,1)S(1)}, bf16[128,1024]{1,0:T(8,128)(2,1)S(1)}, bf16[128,1024]{1,0:T(8,128)(2,1)S(1)}, bf16[128,1024]{1,0:T(8,128)(2,...) custom-call(s32[3]{0:T(128)S(1)} %pad_add_fusion.s_ref, ...), custom_call_target="tpu_custom_call" | custom-call | tf_op jit(solution)/shard_map/attend/pallas_call | solution.py:123
  91.2 2.4 %collective-permute-start.20 = (bf16[2,2,2,128,128]{4,3,2,1,0:T(8,128)(2,1)S(1)}, bf16[2,2,2,128,128]{4,3,2,1,0:T(8,128)(2,1)S(1)}, u32[]{:S(2)}, u32[]{:S(2)}) collective-permute-start(bf16[2,2,2,128,128]{4,3,2,1,0:T(8,128)(2,1)S(1)} %get-tuple-element.29), channel_id=1, source_target_pairs={{0,6},{1,7},{2,0},{3,1},{4,2},{5,3},{6,4},{7,5},{8,14},{9,15},{10,... | collective-permute-start | bytes 786440 | tf_op jit(solution)/shard_map/ppermute | solution.py:153
  94.4 26.9 %attend.3 = (bf16[128,1024]{1,0:T(8,128)(2,1)S(1)}, bf16[128,1024]{1,0:T(8,128)(2,1)S(1)}, bf16[128,1024]{1,0:T(8,128)(2,1)S(1)}, bf16[128,1024]{1,0:T(8,128)(2,...) custom-call(s32[3]{0:T(128)S(1)} %pad_add_fusion.s_ref, ...), custom_call_target="tpu_custom_call" | custom-call | tf_op jit(solution)/shard_map/attend/pallas_call | solution.py:123
  121.2 2.7 %collective-permute-start.25 = (bf16[2,2,2,128,128]{4,3,2,1,0:T(8,128)(2,1)S(1)}, bf16[2,2,2,128,128]{4,3,2,1,0:T(8,128)(2,1)S(1)}, u32[]{:S(2)}, u32[]{:S(2)}) collective-permute-start(bf16[2,2,2,128,128]{4,3,2,1,0:T(8,128)(2,1)S(1)} %get-tuple-element.33), channel_id=1, source_target_pairs={{0,6},{1,7},{2,0},{3,1},{4,2},{5,3},{6,4},{7,5},{8,14},{9,15},{10,... | collective-permute-start | bytes 786440 | tf_op jit(solution)/shard_map/ppermute | solution.py:153
  125.3 14.1 %collective-permute-start.11 = (bf16[2,128,1024]{2,1,0:T(8,128)(2,1)S(1)}, bf16[2,128,1024]{2,1,0:T(8,128)(2,1)S(1)}, u32[]{:S(2)}, u32[]{:S(2)}) collective-permute-start(bf16[2,128,1024]{2,1,0:T(8,128)(2,1)S(1)} %pad_maximum_fusion), channel_id=1, source_target_pairs={{0,1},{1,0},{2,3},{3,2},{4,5},{5,4},{6,7},{7,6},{8,9},{9,8},{10,11... | collective-permute-start | bytes 1572872 | tf_op jit(solution)/shard_map/ppermute | solution.py:153
  139.7 1.3 collective-permute-start.23
  141.1 1.3 collective-permute-start.24
  142.6 1.3 collective-permute-start.28
  143.9 1.8 %collective-permute-done.23 = bf16[2,2,128,128]{3,2,1,0:T(8,128)(2,1)S(1)} collective-permute-done((bf16[2,2,128,128]{3,2,1,0:T(8,128)(2,1)S(1)}, bf16[2,2,128,128]{3,2,1,0:T(8,128)(2,1)S(1)}, u32[]{:S(2)}, u32[]{:S(2)}) %collective-permute-start.23) | collective-permute-done | bytes 131104 | tf_op jit(solution)/shard_map/ppermute | solution.py:153
  145.7 1.3 collective-permute-start.29
  147.0 1.3 collective-permute-done.24
  149.0 5.2 %collective-permute-done.29 = bf16[2,2,128,128]{3,2,1,0:T(8,128)(2,1)S(1)} collective-permute-done((bf16[2,2,128,128]{3,2,1,0:T(8,128)(2,1)S(1)}, bf16[2,2,128,128]{3,2,1,0:T(8,128)(2,1)S(1)}, u32[]{:S(2)}, u32[]{:S(2)}) %collective-permute-start.29) | collective-permute-done | bytes 131104 | tf_op jit(solution)/shard_map/ppermute | solution.py:153
  154.4 5.5 %collective-permute-start.30 = (bf16[2,2,128,128]{3,2,1,0:T(8,128)(2,1)S(1)}, bf16[2,2,128,128]{3,2,1,0:T(8,128)(2,1)S(1)}, u32[]{:S(2)}, u32[]{:S(2)}) collective-permute-start(bf16[2,2,128,128]{3,2,1,0:T(8,128)(2,1)S(1)} %slice_bitcast_fusion.4), channel_id=1, source_target_pairs={{0,1},{1,0},{2,3},{3,2},{4,5},{5,4},{6,7},{7,6},{8,9},{9,8},{10,11... | collective-permute-start | bytes 393224 | tf_op jit(solution)/shard_map/ppermute | solution.py:153
  163.2 1.2 multiply_convert_fusion
  (100 shorter events, 21.3 us)
Async XLA Ops:
  2.9 2.5 %collective-permute-start.2 = (bf16[2,272,128]{2,1,0:T(8,128)(2,1)S(1)}, bf16[2,272,128]{2,1,0:T(8,128)(2,1)S(1)}, u32[]{:S(2)}, u32[]{:S(2)}) collective-permute-start(bf16[2,272,128]{2,1,0:T(8,128)(2,1)S(1)} %get-tuple-element.85), channel_id=1, source_target_pairs={{0,1},{1,0},{2,3},{3,2},{4,5},{5,4},{6,7},{7,6},{8,9},{9,8},{10,11... | collective-permute-start | bytes 417800 | tf_op jit(solution)/shard_map/ppermute | solution.py:153
  6.1 11.6 %collective-permute-start.4 = (bf16[2,2,272,128]{3,2,1,0:T(8,128)(2,1)}, bf16[2,2,272,128]{3,2,1,0:T(8,128)(2,1)S(1)}, u32[]{:S(2)}, u32[]{:S(2)}) collective-permute-start(bf16[2,2,272,128]{3,2,1,0:T(8,128)(2,1)} %pad_maximum_fusion.4), channel_id=1, source_target_pairs={{0,16},{1,17},{2,18},{3,19},{4,20},{5,21},{6,22},{7,23},{8,24},{9,... | collective-permute-start | bytes 835592 | tf_op jit(solution)/shard_map/ppermute | solution.py:153
  12.6 47.2 %collective-permute-start = (bf16[128,2048]{1,0:T(8,128)(2,1)}, bf16[128,2048]{1,0:T(8,128)(2,1)S(1)}, u32[]{:S(2)}, u32[]{:S(2)}) collective-permute-start(bf16[128,2048]{1,0:T(8,128)(2,1)} %dynamic-slice_bitcast_fusion.1), channel_id=1, source_target_pairs={{0,1},{1,0},{2,3},{3,2},{4,5},{5,4},{6,7},{7,6},{8,9},{9,8},{10,11... | collective-permute-start | bytes 1572872 | tf_op jit(solution)/shard_map/ppermute | solution.py:153
  14.0 45.8 %collective-permute-start.1 = (bf16[128,2048]{1,0:T(8,128)(2,1)}, bf16[128,2048]{1,0:T(8,128)(2,1)S(1)}, u32[]{:S(2)}, u32[]{:S(2)}) collective-permute-start(bf16[128,2048]{1,0:T(8,128)(2,1)} %dynamic-slice_bitcast_fusion), channel_id=1, source_target_pairs={{0,1},{1,0},{2,3},{3,2},{4,5},{5,4},{6,7},{7,6},{8,9},{9,8},{10,11... | collective-permute-start | bytes 1572872 | tf_op jit(solution)/shard_map/ppermute | solution.py:153
  14.0 9.6 %collective-permute-start.3 = (bf16[2,2,272,128]{3,2,1,0:T(8,128)(2,1)}, bf16[2,2,272,128]{3,2,1,0:T(8,128)(2,1)S(1)}, u32[]{:S(2)}, u32[]{:S(2)}) collective-permute-start(bf16[2,2,272,128]{3,2,1,0:T(8,128)(2,1)} %pad_maximum_fusion.4), channel_id=1, source_target_pairs={{0,8},{1,9},{2,10},{3,11},{4,12},{5,13},{6,14},{7,15},{8,16},{9,17... | collective-permute-start | bytes 835592 | tf_op jit(solution)/shard_map/ppermute | solution.py:153
  25.3 37.5 %copy-start.4 = (f32[2]{0:T(128)S(1)}, f32[2]{0:T(128)}, u32[]{:S(2)}) copy-start(f32[2]{0:T(128)} %constant.74.clone) | copy-start | bytes 28
  25.3 35.9 %collective-permute-start.5 = (bf16[2,2,272,128]{3,2,1,0:T(8,128)(2,1)}, bf16[2,2,272,128]{3,2,1,0:T(8,128)(2,1)S(1)}, u32[]{:S(2)}, u32[]{:S(2)}) collective-permute-start(bf16[2,2,272,128]{3,2,1,0:T(8,128)(2,1)} %get-tuple-element.78), channel_id=1, source_target_pairs={{0,2},{1,3},{2,4},{3,5},{4,6},{5,7},{6,0},{7,1},{8,10},{9,11},{10,... | collective-permute-start | bytes 835592 | tf_op jit(solution)/shard_map/ppermute | solution.py:153
  27.3 2.6 %collective-permute-start.13 = (f32[1,1]{1,0:T(1,128)}, f32[1,1]{1,0:T(1,128)}, u32[]{:S(2)}, u32[]{:S(2)}) collective-permute-start(f32[1,1]{1,0:T(1,128)} %bitcast.34), channel_id=1, source_target_pairs={{0,1},{1,0},{2,3},{3,2},{4,5},{5,4},{6,7},{7,6},{8,9},{9,8},{10,11... | collective-permute-start | bytes 20 | tf_op jit(solution)/shard_map/ppermute | solution.py:153
  31.1 2.8 %collective-permute-start.14 = (f32[1,1]{1,0:T(1,128)}, f32[1,1]{1,0:T(1,128)}, u32[]{:S(2)}, u32[]{:S(2)}) collective-permute-start(f32[1,1]{1,0:T(1,128)} %add.166), channel_id=1, source_target_pairs={{0,32},{32,0},{64,96},{96,64},{1,33},{33,1},{65,97},{97,65},{2,34}... | collective-permute-start | bytes 20 | tf_op jit(solution)/shard_map/ppermute | solution.py:162
  34.5 2.4 %collective-permute-start.15 = (f32[1,1]{1,0:T(1,128)}, f32[1,1]{1,0:T(1,128)}, u32[]{:S(2)}, u32[]{:S(2)}) collective-permute-start(f32[1,1]{1,0:T(1,128)} %add.167), channel_id=1, source_target_pairs={{0,2},{1,3},{2,0},{3,1},{4,6},{5,7},{6,4},{7,5},{8,10},{9,11},{10,... | collective-permute-start | bytes 20 | tf_op jit(solution)/shard_map/ppermute | solution.py:153
  37.6 3.1 %collective-permute-start.16 = (f32[1,1]{1,0:T(1,128)}, f32[1,1]{1,0:T(1,128)}, u32[]{:S(2)}, u32[]{:S(2)}) collective-permute-start(f32[1,1]{1,0:T(1,128)} %add.168), channel_id=1, source_target_pairs={{0,8},{1,9},{2,10},{3,11},{4,12},{5,13},{6,14},{7,15},{8,0},{9,1},... | collective-permute-start | bytes 20 | tf_op jit(solution)/shard_map/ppermute | solution.py:153
  41.3 3.9 %collective-permute-start.17 = (f32[1,1]{1,0:T(1,128)}, f32[1,1]{1,0:T(1,128)}, u32[]{:S(2)}, u32[]{:S(2)}) collective-permute-start(f32[1,1]{1,0:T(1,128)} %add.169), channel_id=1, source_target_pairs={{0,64},{32,96},{64,0},{96,32},{1,65},{33,97},{65,1},{97,33},{2,66}... | collective-permute-start | bytes 20 | tf_op jit(solution)/shard_map/ppermute | solution.py:162
  45.8 3.9 %collective-permute-start.18 = (f32[1,1]{1,0:T(1,128)}, f32[1,1]{1,0:T(1,128)}, u32[]{:S(2)}, u32[]{:S(2)}) collective-permute-start(f32[1,1]{1,0:T(1,128)} %add.170), channel_id=1, source_target_pairs={{0,4},{1,5},{2,6},{3,7},{4,0},{5,1},{6,2},{7,3},{8,12},{9,13},{10,... | collective-permute-start | bytes 20 | tf_op jit(solution)/shard_map/ppermute | solution.py:153
  50.4 8.3 %collective-permute-start.19 = (f32[1,1]{1,0:T(1,128)}, f32[1,1]{1,0:T(1,128)}, u32[]{:S(2)}, u32[]{:S(2)}) collective-permute-start(f32[1,1]{1,0:T(1,128)} %add.171), channel_id=1, source_target_pairs={{0,16},{1,17},{2,18},{3,19},{4,20},{5,21},{6,22},{7,23},{8,24},{9,... | collective-permute-start | bytes 20 | tf_op jit(solution)/shard_map/ppermute | solution.py:153
  54.2 8.7 %collective-permute-start.6 = (bf16[2,2,272,128]{3,2,1,0:T(8,128)(2,1)}, bf16[2,2,272,128]{3,2,1,0:T(8,128)(2,1)}, u32[]{:S(2)}, u32[]{:S(2)}) collective-permute-start(bf16[2,2,272,128]{3,2,1,0:T(8,128)(2,1)} %get-tuple-element.79), channel_id=1, source_target_pairs={{0,4},{1,5},{2,6},{3,7},{4,0},{5,1},{6,2},{7,3},{8,12},{9,13},{10,... | collective-permute-start | bytes 835592 | tf_op jit(solution)/shard_map/ppermute | solution.py:153
  58.7 5.7 %collective-permute-start.7 = (bf16[2,2,272,128]{3,2,1,0:T(8,128)(2,1)}, bf16[2,2,272,128]{3,2,1,0:T(8,128)(2,1)}, u32[]{:S(2)}, u32[]{:S(2)}) collective-permute-start(bf16[2,2,272,128]{3,2,1,0:T(8,128)(2,1)} %get-tuple-element.77), channel_id=1, source_target_pairs={{0,6},{1,7},{2,0},{3,1},{4,2},{5,3},{6,4},{7,5},{8,14},{9,15},{10,... | collective-permute-start | bytes 835592 | tf_op jit(solution)/shard_map/ppermute | solution.py:153
  59.8 34.6 %collective-permute-start.10 = (bf16[2,2,272,128]{3,2,1,0:T(8,128)(2,1)}, bf16[2,2,272,128]{3,2,1,0:T(8,128)(2,1)S(1)}, u32[]{:S(2)}, u32[]{:S(2)}) collective-permute-start(bf16[2,2,272,128]{3,2,1,0:T(8,128)(2,1)} %get-tuple-element.74), channel_id=1, source_target_pairs={{0,6},{1,7},{2,0},{3,1},{4,2},{5,3},{6,4},{7,5},{8,14},{9,15},{10,... | collective-permute-start | bytes 835592 | tf_op jit(solution)/shard_map/ppermute | solution.py:153
  59.9 34.5 %collective-permute-start.8 = (bf16[2,2,272,128]{3,2,1,0:T(8,128)(2,1)}, bf16[2,2,272,128]{3,2,1,0:T(8,128)(2,1)}, u32[]{:S(2)}, u32[]{:S(2)}) collective-permute-start(bf16[2,2,272,128]{3,2,1,0:T(8,128)(2,1)} %get-tuple-element.75), channel_id=1, source_target_pairs={{0,2},{1,3},{2,4},{3,5},{4,6},{5,7},{6,0},{7,1},{8,10},{9,11},{10,... | collective-permute-start | bytes 835592 | tf_op jit(solution)/shard_map/ppermute | solution.py:153
  61.3 33.1 %collective-permute-start.9 = (bf16[2,2,272,128]{3,2,1,0:T(8,128)(2,1)}, bf16[2,2,272,128]{3,2,1,0:T(8,128)(2,1)}, u32[]{:S(2)}, u32[]{:S(2)}) collective-permute-start(bf16[2,2,272,128]{3,2,1,0:T(8,128)(2,1)} %get-tuple-element.76), channel_id=1, source_target_pairs={{0,4},{1,5},{2,6},{3,7},{4,0},{5,1},{6,2},{7,3},{8,12},{9,13},{10,... | collective-permute-start | bytes 835592 | tf_op jit(solution)/shard_map/ppermute | solution.py:153
  91.2 33.8 %collective-permute-start.20 = (bf16[2,2,2,128,128]{4,3,2,1,0:T(8,128)(2,1)S(1)}, bf16[2,2,2,128,128]{4,3,2,1,0:T(8,128)(2,1)S(1)}, u32[]{:S(2)}, u32[]{:S(2)}) collective-permute-start(bf16[2,2,2,128,128]{4,3,2,1,0:T(8,128)(2,1)S(1)} %get-tuple-element.29), channel_id=1, source_target_pairs={{0,6},{1,7},{2,0},{3,1},{4,2},{5,3},{6,4},{7,5},{8,14},{9,15},{10,... | collective-permute-start | bytes 786440 | tf_op jit(solution)/shard_map/ppermute | solution.py:153
  93.6 31.7 %collective-permute-start.21 = (bf16[2,2,2,128,128]{4,3,2,1,0:T(8,128)(2,1)S(1)}, bf16[2,2,2,128,128]{4,3,2,1,0:T(8,128)(2,1)S(1)}, u32[]{:S(2)}, u32[]{:S(2)}) collective-permute-start(bf16[2,2,2,128,128]{4,3,2,1,0:T(8,128)(2,1)S(1)} %get-tuple-element.30), channel_id=1, source_target_pairs={{0,4},{1,5},{2,6},{3,7},{4,0},{5,1},{6,2},{7,3},{8,12},{9,13},{10,... | collective-permute-start | bytes 786440 | tf_op jit(solution)/shard_map/ppermute | solution.py:153
  94.3 45.1 %collective-permute-start.22 = (bf16[2,2,2,128,128]{4,3,2,1,0:T(8,128)(2,1)S(1)}, bf16[2,2,2,128,128]{4,3,2,1,0:T(8,128)(2,1)S(1)}, u32[]{:S(2)}, u32[]{:S(2)}) collective-permute-start(bf16[2,2,2,128,128]{4,3,2,1,0:T(8,128)(2,1)S(1)} %get-tuple-element.31), channel_id=1, source_target_pairs={{0,2},{1,3},{2,4},{3,5},{4,6},{5,7},{6,0},{7,1},{8,10},{9,11},{10,... | collective-permute-start | bytes 786440 | tf_op jit(solution)/shard_map/ppermute | solution.py:153
  121.2 18.5 %collective-permute-start.25 = (bf16[2,2,2,128,128]{4,3,2,1,0:T(8,128)(2,1)S(1)}, bf16[2,2,2,128,128]{4,3,2,1,0:T(8,128)(2,1)S(1)}, u32[]{:S(2)}, u32[]{:S(2)}) collective-permute-start(bf16[2,2,2,128,128]{4,3,2,1,0:T(8,128)(2,1)S(1)} %get-tuple-element.33), channel_id=1, source_target_pairs={{0,6},{1,7},{2,0},{3,1},{4,2},{5,3},{6,4},{7,5},{8,14},{9,15},{10,... | collective-permute-start | bytes 786440 | tf_op jit(solution)/shard_map/ppermute | solution.py:153
  123.9 17.1 %collective-permute-start.26 = (bf16[2,2,2,128,128]{4,3,2,1,0:T(8,128)(2,1)S(1)}, bf16[2,2,2,128,128]{4,3,2,1,0:T(8,128)(2,1)S(1)}, u32[]{:S(2)}, u32[]{:S(2)}) collective-permute-start(bf16[2,2,2,128,128]{4,3,2,1,0:T(8,128)(2,1)S(1)} %get-tuple-element.34), channel_id=1, source_target_pairs={{0,4},{1,5},{2,6},{3,7},{4,0},{5,1},{6,2},{7,3},{8,12},{9,13},{10,... | collective-permute-start | bytes 786440 | tf_op jit(solution)/shard_map/ppermute | solution.py:153
  125.1 17.3 %collective-permute-start.27 = (bf16[2,2,2,128,128]{4,3,2,1,0:T(8,128)(2,1)S(1)}, bf16[2,2,2,128,128]{4,3,2,1,0:T(8,128)(2,1)S(1)}, u32[]{:S(2)}, u32[]{:S(2)}) collective-permute-start(bf16[2,2,2,128,128]{4,3,2,1,0:T(8,128)(2,1)S(1)} %get-tuple-element.35), channel_id=1, source_target_pairs={{0,2},{1,3},{2,4},{3,5},{4,6},{5,7},{6,0},{7,1},{8,10},{9,11},{10,... | collective-permute-start | bytes 786440 | tf_op jit(solution)/shard_map/ppermute | solution.py:153
  125.3 37.6 %collective-permute-start.11 = (bf16[2,128,1024]{2,1,0:T(8,128)(2,1)S(1)}, bf16[2,128,1024]{2,1,0:T(8,128)(2,1)S(1)}, u32[]{:S(2)}, u32[]{:S(2)}) collective-permute-start(bf16[2,128,1024]{2,1,0:T(8,128)(2,1)S(1)} %pad_maximum_fusion), channel_id=1, source_target_pairs={{0,1},{1,0},{2,3},{3,2},{4,5},{5,4},{6,7},{7,6},{8,9},{9,8},{10,11... | collective-permute-start | bytes 1572872 | tf_op jit(solution)/shard_map/ppermute | solution.py:153
  139.4 23.5 %collective-permute-start.12 = (bf16[2,128,1024]{2,1,0:T(8,128)(2,1)S(1)}, bf16[2,128,1024]{2,1,0:T(8,128)(2,1)S(1)}, u32[]{:S(2)}, u32[]{:S(2)}) collective-permute-start(bf16[2,128,1024]{2,1,0:T(8,128)(2,1)S(1)} %pad_maximum_fusion.1), channel_id=1, source_target_pairs={{0,1},{1,0},{2,3},{3,2},{4,5},{5,4},{6,7},{7,6},{8,9},{9,8},{10,11... | collective-permute-start | bytes 1572872 | tf_op jit(solution)/shard_map/ppermute | solution.py:153
  139.7 6.0 %collective-permute-start.23 = (bf16[2,2,128,128]{3,2,1,0:T(8,128)(2,1)S(1)}, bf16[2,2,128,128]{3,2,1,0:T(8,128)(2,1)S(1)}, u32[]{:S(2)}, u32[]{:S(2)}) collective-permute-start(bf16[2,2,128,128]{3,2,1,0:T(8,128)(2,1)S(1)} %get-tuple-element.44), channel_id=1, source_target_pairs={{8,0},{9,1},{10,2},{11,3},{12,4},{13,5},{14,6},{15,7},{16,8},{17,9... | collective-permute-start | bytes 393224 | tf_op jit(solution)/shard_map/ppermute | solution.py:153
  141.1 7.2 %collective-permute-start.24 = (bf16[2,2,128,128]{3,2,1,0:T(8,128)(2,1)S(1)}, bf16[2,2,128,128]{3,2,1,0:T(8,128)(2,1)S(1)}, u32[]{:S(2)}, u32[]{:S(2)}) collective-permute-start(bf16[2,2,128,128]{3,2,1,0:T(8,128)(2,1)S(1)} %get-tuple-element.45), channel_id=1, source_target_pairs={{16,0},{17,1},{18,2},{19,3},{20,4},{21,5},{22,6},{23,7},{24,8},{25... | collective-permute-start | bytes 393224 | tf_op jit(solution)/shard_map/ppermute | solution.py:153
  142.6 6.3 %collective-permute-start.28 = (bf16[2,2,128,128]{3,2,1,0:T(8,128)(2,1)S(1)}, bf16[2,2,128,128]{3,2,1,0:T(8,128)(2,1)S(1)}, u32[]{:S(2)}, u32[]{:S(2)}) collective-permute-start(bf16[2,2,128,128]{3,2,1,0:T(8,128)(2,1)S(1)} %get-tuple-element.46), channel_id=1, source_target_pairs={{8,0},{9,1},{10,2},{11,3},{12,4},{13,5},{14,6},{15,7},{16,8},{17,9... | collective-permute-start | bytes 393224 | tf_op jit(solution)/shard_map/ppermute | solution.py:153
  145.7 8.5 %collective-permute-start.29 = (bf16[2,2,128,128]{3,2,1,0:T(8,128)(2,1)S(1)}, bf16[2,2,128,128]{3,2,1,0:T(8,128)(2,1)S(1)}, u32[]{:S(2)}, u32[]{:S(2)}) collective-permute-start(bf16[2,2,128,128]{3,2,1,0:T(8,128)(2,1)S(1)} %get-tuple-element.47), channel_id=1, source_target_pairs={{16,0},{17,1},{18,2},{19,3},{20,4},{21,5},{22,6},{23,7},{24,8},{25... | collective-permute-start | bytes 393224 | tf_op jit(solution)/shard_map/ppermute | solution.py:153
  154.4 6.5 %collective-permute-start.30 = (bf16[2,2,128,128]{3,2,1,0:T(8,128)(2,1)S(1)}, bf16[2,2,128,128]{3,2,1,0:T(8,128)(2,1)S(1)}, u32[]{:S(2)}, u32[]{:S(2)}) collective-permute-start(bf16[2,2,128,128]{3,2,1,0:T(8,128)(2,1)S(1)} %slice_bitcast_fusion.4), channel_id=1, source_target_pairs={{0,1},{1,0},{2,3},{3,2},{4,5},{5,4},{6,7},{7,6},{8,9},{9,8},{10,11... | collective-permute-start | bytes 393224 | tf_op jit(solution)/shard_map/ppermute | solution.py:153
  (4 other events, 24.4 us)

commit v2 on v1

--- a/solution.py
+++ b/solution.py
@@ -20,8 +20,8 @@
     return lax.dot_general(a, b, NT, preferred_element_type=F32)
 
 
-def attend_kernel(s_ref, qo_ref, qs_ref, go_ref, gs_ref, own_ref, za_ref, zc_ref, y1_ref, y2_ref, y3_ref,
-                  oo_ref, os_ref, dqo_ref, dqs_ref, p1_ref, p2_ref, p3_ref, loc_ref,
+def attend_kernel(s_ref, qo_ref, qs_ref, go_ref, gs_ref, own_ref, za_ref, zc_ref, y1_ref, y2_ref, y3_ref, tally_ref,
+                  oo_ref, os_ref, dqo_ref, dqs_ref, p1_ref, p2_ref, p3_ref, loc_ref, cnt_ref,
                   kk, vv, kt, vt, bias, sc, pp, ds, dka, dva):
     core, z, y = s_ref[0], s_ref[1], s_ref[2]
     chip = 4 * z + y
@@ -55,6 +55,10 @@
                 first = jnp.where(idx >= 0, first, 128)
                 ok = key >= first
             bias[r0:r0 + 128] = jnp.where(ok, 0.0, NEG)
+    tally = tally_ref[...]
+    for ref in (y1_ref, y2_ref, y3_ref):
+        tally = tally + 32.0 * ref[0, 0, 258:259].astype(F32) + ref[0, 0, 259:260].astype(F32)
+    cnt_ref[...] = tally
     dka[...] = jnp.zeros_like(dka)
     dva[...] = jnp.zeros_like(dva)
 
@@ -110,7 +114,7 @@
                 ref[(b - 3) % 2, o, 1] = dva[rows].astype(BF)
 
 
-def attend(scal, j, q, qs, g, gs, own, za, zc, y1, y2, y3):
+def attend(scal, j, q, qs, g, gs, own, za, zc, y1, y2, y3, tally):
     wide = lambda f: pl.BlockSpec((128, 1024), f)
     whole = lambda a: pl.BlockSpec(a.shape, lambda i, s, n=a.ndim: (0,) * n)
     mine = wide(lambda i, s: (0, s[0] * 2 + j))
@@ -118,7 +122,7 @@
     rows = jax.ShapeDtypeStruct((128, 1024), BF)
     part = jax.ShapeDtypeStruct((2, 2, 2, 128, 128), BF)
     loc = jax.ShapeDtypeStruct((3, 2, 2, 128, 128), F32)
-    outs = [rows] * 4 + [part] * 3 + [loc]
+    outs = [rows] * 4 + [part] * 3 + [loc, jax.ShapeDtypeStruct((8, 128), F32)]
     n = NB * 256
     return pl.pallas_call(
         attend_kernel,
@@ -126,7 +130,7 @@
         grid_spec=pltpu.PrefetchScalarGridSpec(
             num_scalar_prefetch=1,
             grid=(1,),
-            in_specs=[mine, other, mine, other] + [whole(a) for a in (own, za, zc, y1, y2, y3)],
+            in_specs=[mine, other, mine, other] + [whole(a) for a in (own, za, zc, y1, y2, y3, tally)],
             out_specs=[whole(o) for o in outs],
             scratch_shapes=[
                 pltpu.VMEM((n, 128), BF), pltpu.VMEM((n, 128), BF), pltpu.VMEM((128, n), BF), pltpu.VMEM((128, n), BF),
@@ -135,8 +139,9 @@
             ],
         ),
         compiler_params=pltpu.CompilerParams(vmem_limit_bytes=48 * 2**20),
+        cost_estimate=pl.CostEstimate(flops=15 * 2**30, bytes_accessed=4 * 2**20, transcendentals=5 * 2**20),
         name="attend",
-    )(scal, q, qs, g, gs, own, za, zc, y1, y2, y3)
+    )(scal, q, qs, g, gs, own, za, zc, y1, y2, y3, tally)
 
 
 def shard(queries, keys, values, out_grad, segment_ids, loss_mask):
@@ -144,24 +149,17 @@
     core, y, z = me % 2, me // 2 % 4, me // 8
     q, k, v, g = queries[0], keys[0], values[0], out_grad[0]
 
-    def send(x, target):
+    def send(x, target, turn=False):
         pairs = []
         for i in range(32):
             zz, yy, cc = target(i // 8, i // 2 % 4, i % 2)
-            if 0 <= zz < 4:
-                pairs.append((i, (zz * 4 + yy % 4) * 2 + cc % 2))
+            if turn or 0 <= zz < 4:
+                pairs.append((i, (zz % 4 * 4 + yy % 4) * 2 + cc % 2))
         return lax.ppermute(x, "ctx", pairs)
 
     swap = lambda x: send(x, lambda z, y, c: (z, y, c + 1))
-    along_z = lambda x, a: send(x, lambda z, y, c: (z + a, y, c))
+    along_z = lambda x, a, turn=False: send(x, lambda z, y, c: (z + a, y, c), turn)
     along_y = lambda x, s: send(x, lambda z, y, c: (z, y + s, c))
-
-    counted = jnp.sum(loss_mask.astype(F32), axis=1, keepdims=True)
-    counted = counted + swap(counted)
-    for step in (1, 2):
-        counted = counted + lax.ppermute(counted, "dp", [(i, i ^ step) for i in range(4)])
-        counted = counted + send(counted, lambda z, y, c: (z, y ^ step, c))
-        counted = counted + send(counted, lambda z, y, c: (z ^ step, y, c))
 
     info = jnp.concatenate([segment_ids.astype(BF), loss_mask.astype(BF), jnp.zeros((14, 128), BF)], axis=0)
 
@@ -171,18 +169,27 @@
 
     own = jnp.stack([payload(core), swap(payload(1 - core))], axis=1)
     half = lambda a, c: lax.dynamic_slice(a, (0, c * 2048), (128, 2048))
-    za, zc = along_z(own, 1), along_z(own, 2)
+    za, zc = zip(*[(along_z(own[j], 1, True), along_z(own[j], 2)) for j in range(2)])
     qs, gs = swap(half(q, 1 - core)), swap(half(g, 1 - core))
     scal = jnp.stack([core, z, y]).astype(jnp.int32)
 
+    counted = jnp.broadcast_to(jnp.sum(za[0][:, 257].astype(F32)), (8, 128))
+    for step in (1, 2):
+        counted = counted + lax.ppermute(counted, "dp", [(i, i ^ step) for i in range(4)])
+    high = jnp.floor(counted[:1] / 32)
+    digits = jnp.concatenate([high, counted[:1] - 32 * high]).astype(BF)
+
     ys = []
     for j in range(2):
+        above = za[j] if j == 0 else za[j].at[0, 258:260].set(digits)
         ys.append([
-            along_y(jnp.stack([za[j], jnp.where(y + s < 4, own[j], zc[j])]), s) for s in (1, 2, 3)
+            along_y(jnp.stack([above, jnp.where(y + s < 4, own[j], zc[j])]), s) for s in (1, 2, 3)
         ])
     rows_out, grads = [], []
     for j in range(2):
-        oo, os, dqo, dqs, p1, p2, p3, loc = attend(scal, j, q, qs, g, gs, own[j], za[j], zc[j], *ys[j])
+        oo, os, dqo, dqs, p1, p2, p3, loc, tally = attend(
+            scal, j, q, qs, g, gs, own[j], za[j], zc[j], *ys[j], counted
+        )
         rows_out.append((oo, dqo, swap(jnp.stack([os, dqs]))))
         got = [along_y(p, -s) for s, p in ((1, p1), (2, p2), (3, p3))]
         got = [a.astype(F32) for a in got]
@@ -193,6 +200,9 @@
             here = here + jnp.where(y + s < 4, a[1], 0.0)
             back_c = back_c + jnp.where(y + s < 4, 0.0, a[1])
         grads.append(here + along_z(back_a.astype(BF), -1).astype(F32) + along_z(back_c.astype(BF), -2).astype(F32))
+    counted = tally
+    for step in (1, 2):
+        counted = counted + send(counted, lambda z, y, c: (z ^ step, y, c))
     scale = float(lax.axis_size("dp") * 4096) / counted[0, 0]
     total = jnp.stack(grads) * (jnp.array([1.0 / math.sqrt(128), 1.0], F32)[None, None, :, None, None] * scale)
     total = total.astype(BF)

time: 166 us -> 146 us (0.88)
  starting transfers between devices: 68.6 us -> 54.5 us
  waiting for transfers between devices: 21.9 us -> 14 us
  local copies, waits for them, and re-layouts: 6.41 us -> 10.8 us
  between operations: 6.22 us -> 1.89 us
  other arithmetic: 8.88 us -> 11.3 us
    ppermute x29 -> x28, starting transfers between devices: 63 us -> 50.4 us  [send(): return lax.ppermute(x, 'ctx', pairs)]
    ppermute x29 -> x28, waiting for transfers between devices: 20.7 us -> 13.8 us  [send(): return lax.ppermute(x, 'ctx', pairs)]
    scatter x0 -> x1, local copies, waits for them, and re-layouts: none -> 2.55 us  [shard(): above = za[j] if j == 0 else za[j].at[0, 258:260].set(digits)]
    another operation x4 -> x7, other arithmetic: 3.61 us -> 5.49 us  [the longest x5 4.78 us: shard(): jnp.stack([above, jnp.where(y + s < 4, own[j], zc[j])])]
  transfers between devices with their start and end apart: 31 -> 30, of which waited for: 15 -> 10; matrix products, arithmetic and copies ran while one was open for 6% -> 12% of each run, Pallas kernels for 32% -> 37%
where the time goes in v2:
time: 146 us
  starting transfers between devices  54.5 us (37%)
  Pallas kernels  53.5 us (37%)
  waiting for transfers between devices  14 us (10%)
  other arithmetic  11.3 us (8%)
  local copies, waits for them, and re-layouts  10.8 us (7%)
  between operations  1.89 us (1%)
    pallas_call x2, Pallas kernels, attend(): pl.pallas_call(attend_kernel, out_shape=outs, grid_spec=pltpu.PrefetchSca...  53.5 us
    ppermute x28, starting transfers between devices, send(): return lax.ppermute(x, 'ctx', pairs)  50.4 us
    ppermute x28, waiting for transfers between devices, send(): return lax.ppermute(x, 'ctx', pairs)  13.8 us
    another operation x5, other arithmetic, shard(): jnp.stack([above, jnp.where(y + s < 4, own[j], zc[j])])  4.78 us
    ppermute x2, starting transfers between devices, shard(): lax.ppermute(counted, 'dp', [(i, i ^ step) for i in range(4)])  4.11 us
  transfers between devices with their start and end apart: 30, of which 10 were waited for; matrix products, arithmetic and copies ran while one was open for 12% of the time, Pallas kernels for 37%

profile of v2, /device:TPU:1, one launch (start us, length us, event | category | flops | bytes accessed | tf_op | source)
XLA Modules:
  0.0 145.9 jit_solution(8647799989484537138)
XLA Ops:
  3.0 1.5 %collective-permute-start.2 = (bf16[2,272,128]{2,1,0:T(8,128)(2,1)S(1)}, bf16[2,272,128]{2,1,0:T(8,128)(2,1)S(1)}, u32[]{:S(2)}, u32[]{:S(2)}) collective-permute-start(bf16[2,272,128]{2,1,0:T(8,128)(2,1)S(1)} %get-tuple-element.88), channel_id=1, source_target_pairs={{0,1},{1,0},{2,3},{3,2},{4,5},{5,4},{6,7},{7,6},{8,9},{9,8},{10,11... | collective-permute-start | bytes 417800 | tf_op jit(solution)/shard_map/ppermute | solution.py:158
  7.4 1.8 %collective-permute-start.3 = (bf16[2,272,128]{2,1,0:T(8,128)(2,1)S(1)}, bf16[2,272,128]{2,1,0:T(8,128)(2,1)S(1)}, u32[]{:S(2)}, u32[]{:S(2)}) collective-permute-start(bf16[2,272,128]{2,1,0:T(8,128)(2,1)S(1)} %get-tuple-element.72.own_ref), channel_id=1, source_target_pairs={{0,8},{1,9},{2,10},{3,11},{4,12},{5,13},{6,14},{7,15},{8,16},{9,17... | collective-permute-start | bytes 417800 | tf_op jit(solution)/shard_map/ppermute | solution.py:158
  9.8 5.2 %collective-permute-start.4 = (bf16[2,272,128]{2,1,0:T(8,128)(2,1)S(1)}, bf16[2,272,128]{2,1,0:T(8,128)(2,1)S(1)}, u32[]{:S(2)}, u32[]{:S(2)}) collective-permute-start(bf16[2,272,128]{2,1,0:T(8,128)(2,1)S(1)} %get-tuple-element.72.own_ref), channel_id=1, source_target_pairs={{0,16},{1,17},{2,18},{3,19},{4,20},{5,21},{6,22},{7,23},{8,24},{9,... | collective-permute-start | bytes 417800 | tf_op jit(solution)/shard_map/ppermute | solution.py:158
  15.3 3.0 %collective-permute-start.11 = (bf16[2,272,128]{2,1,0:T(8,128)(2,1)S(1)}, bf16[2,272,128]{2,1,0:T(8,128)(2,1)S(1)}, u32[]{:S(2)}, u32[]{:S(2)}) collective-permute-start(bf16[2,272,128]{2,1,0:T(8,128)(2,1)S(1)} %get-tuple-element.71.own_ref), channel_id=1, source_target_pairs={{0,16},{1,17},{2,18},{3,19},{4,20},{5,21},{6,22},{7,23},{8,24},{9,... | collective-permute-start | bytes 417800 | tf_op jit(solution)/shard_map/ppermute | solution.py:158
  19.6 1.3 collective-permute-start.8
  22.1 1.3 collective-permute-start.5
  24.1 2.8 %collective-permute-start.9 = (f32[8,128]{1,0:T(8,128)S(1)}, f32[8,128]{1,0:T(8,128)S(1)}, u32[]{:S(2)}, u32[]{:S(2)}) collective-permute-start(f32[8,128]{1,0:T(8,128)S(1)} %broadcast_add_fusion), channel_id=1, source_target_pairs={{0,64},{32,96},{64,0},{96,32},{1,65},{33,97},{65,1},{97,33},{2,66}... | collective-permute-start | bytes 12296 | tf_op jit(solution)/shard_map/ppermute | solution.py:178
  27.7 2.6 %collective-permute-start.6 = (bf16[2,2,272,128]{3,2,1,0:T(8,128)(2,1)}, bf16[2,2,272,128]{3,2,1,0:T(8,128)(2,1)S(1)}, u32[]{:S(2)}, u32[]{:S(2)}) collective-permute-start(bf16[2,2,272,128]{3,2,1,0:T(8,128)(2,1)} %get-tuple-element.82), channel_id=1, source_target_pairs={{0,4},{1,5},{2,6},{3,7},{4,0},{5,1},{6,2},{7,3},{8,12},{9,13},{10,... | collective-permute-start | bytes 835592 | tf_op jit(solution)/shard_map/ppermute | solution.py:158
  31.0 1.1 collective-permute-start.7
  32.7 1.8 %fusion.16 = bf16[1,1,2,128]{3,2,1,0:T(2,128)(2,1)S(1)} fusion(pred[]{:T(512)} %and_reduce_fusion, bf16[2,272,128]{2,1,0:T(8,128)(2,1)S(1)} %collective-permute-done.10.za_ref, s32[]{:T(128)} %bitcast.26, s32[]{:T(128)} %bitcast.27, bf16[1,1,128]{2,1,0:T(2,128)(2,1)S(1)} %get-tuple-element.91, bf16[1,1,128]{2,1,0:T(2,128)(2,1)S(1)} %get-tuple-element.90), kind=kLoop, calls=%fused_computation.79 | loop fusion | flops 1280 | bytes 1545 | tf_op jit(solution)/shard_map/stack | solution.py:186
  34.6 2.6 %scatter.4 = bf16[1,2,272,128]{3,2,1,0:T(8,128)(2,1)} dynamic-update-slice(bf16[1,2,272,128]{3,2,1,0:T(8,128)(2,1)} %copy.30, bf16[1,1,2,128]{3,2,1,0:T(2,128)(2,1)S(1)} %fusion.16, s32[]{:T(128)} %constant.86.clone.1, s32[]{:T(128)} %bitcast.26, s32[]{:T(128)} %bitcast.27, s32[]{:T(128)} %constant.86.clone.1) | dynamic-update-slice | bytes 1028 | tf_op jit(solution)/shard_map/scatter | solution.py:184
  37.1 1.2 pad_maximum_fusion.7
  39.6 1.9 %collective-permute-start.14 = (bf16[2,2,272,128]{3,2,1,0:T(8,128)(2,1)S(1)}, bf16[2,2,272,128]{3,2,1,0:T(8,128)(2,1)S(1)}, u32[]{:S(2)}, u32[]{:S(2)}) collective-permute-start(bf16[2,2,272,128]{3,2,1,0:T(8,128)(2,1)S(1)} %get-tuple-element.78), channel_id=1, source_target_pairs={{0,6},{1,7},{2,0},{3,1},{4,2},{5,3},{6,4},{7,5},{8,14},{9,15},{10,... | collective-permute-start | bytes 835592 | tf_op jit(solution)/shard_map/ppermute | solution.py:158
  42.2 26.8 %attend.2 = (bf16[128,1024]{1,0:T(8,128)(2,1)S(1)}, bf16[128,1024]{1,0:T(8,128)(2,1)S(1)}, bf16[128,1024]{1,0:T(8,128)(2,1)S(1)}, bf16[128,1024]{1,0:T(8,128)(2,...) custom-call(s32[3]{0:T(128)S(1)} %pad_add_fusion.s_ref, ...), custom_call_target="tpu_custom_call" | custom-call | flops 16106127360 | bytes 4194304 | tf_op jit(solution)/shard_map/attend/pallas_call | solution.py:127
  69.0 3.5 %collective-permute-start.19 = (bf16[2,2,2,128,128]{4,3,2,1,0:T(8,128)(2,1)S(1)}, bf16[2,2,2,128,128]{4,3,2,1,0:T(8,128)(2,1)S(1)}, u32[]{:S(2)}, u32[]{:S(2)}) collective-permute-start(bf16[2,2,2,128,128]{4,3,2,1,0:T(8,128)(2,1)S(1)} %get-tuple-element.43), channel_id=1, source_target_pairs={{0,6},{1,7},{2,0},{3,1},{4,2},{5,3},{6,4},{7,5},{8,14},{9,15},{10,... | collective-permute-start | bytes 786440 | tf_op jit(solution)/shard_map/ppermute | solution.py:158
  72.5 2.7 %collective-permute-start.20 = (bf16[2,2,2,128,128]{4,3,2,1,0:T(8,128)(2,1)S(1)}, bf16[2,2,2,128,128]{4,3,2,1,0:T(8,128)(2,1)S(1)}, u32[]{:S(2)}, u32[]{:S(2)}) collective-permute-start(bf16[2,2,2,128,128]{4,3,2,1,0:T(8,128)(2,1)S(1)} %get-tuple-element.44), channel_id=1, source_target_pairs={{0,4},{1,5},{2,6},{3,7},{4,0},{5,1},{6,2},{7,3},{8,12},{9,13},{10,... | collective-permute-start | bytes 786440 | tf_op jit(solution)/shard_map/ppermute | solution.py:158
  75.7 26.7 %attend.3 = (bf16[128,1024]{1,0:T(8,128)(2,1)S(1)}, bf16[128,1024]{1,0:T(8,128)(2,1)S(1)}, bf16[128,1024]{1,0:T(8,128)(2,1)S(1)}, bf16[128,1024]{1,0:T(8,128)(2,...) custom-call(s32[3]{0:T(128)S(1)} %pad_add_fusion.s_ref, ...), custom_call_target="tpu_custom_call" | custom-call | flops 16106127360 | bytes 4194304 | tf_op jit(solution)/shard_map/attend/pallas_call | solution.py:127
  102.4 2.7 %collective-permute-start.24 = (bf16[2,2,2,128,128]{4,3,2,1,0:T(8,128)(2,1)S(1)}, bf16[2,2,2,128,128]{4,3,2,1,0:T(8,128)(2,1)S(1)}, u32[]{:S(2)}, u32[]{:S(2)}) collective-permute-start(bf16[2,2,2,128,128]{4,3,2,1,0:T(8,128)(2,1)S(1)} %get-tuple-element.47), channel_id=1, source_target_pairs={{0,6},{1,7},{2,0},{3,1},{4,2},{5,3},{6,4},{7,5},{8,14},{9,15},{10,... | collective-permute-start | bytes 786440 | tf_op jit(solution)/shard_map/ppermute | solution.py:158
  105.1 2.6 %collective-permute-start.17 = (f32[8,128]{1,0:T(8,128)S(1)}, f32[8,128]{1,0:T(8,128)S(1)}, u32[]{:S(2)}, u32[]{:S(2)}) collective-permute-start(f32[8,128]{1,0:T(8,128)S(1)} %get-tuple-element.41), channel_id=1, source_target_pairs={{0,8},{1,9},{2,10},{3,11},{4,12},{5,13},{6,14},{7,15},{8,0},{9,1},... | collective-permute-start | bytes 12296 | tf_op jit(solution)/shard_map/ppermute | solution.py:158
  108.7 1.7 %collective-permute-start.18 = (f32[8,128]{1,0:T(8,128)S(1)}, f32[8,128]{1,0:T(8,128)S(1)}, u32[]{:S(2)}, u32[]{:S(2)}) collective-permute-start(f32[8,128]{1,0:T(8,128)S(1)} %add.161), channel_id=1, source_target_pairs={{0,16},{1,17},{2,18},{3,19},{4,20},{5,21},{6,22},{7,23},{8,24},{9,... | collective-permute-start | bytes 12296 | tf_op jit(solution)/shard_map/ppermute | solution.py:158
  110.3 2.3 %collective-permute-done.18 = f32[8,128]{1,0:T(8,128)S(1)} collective-permute-done((f32[8,128]{1,0:T(8,128)S(1)}, f32[8,128]{1,0:T(8,128)S(1)}, u32[]{:S(2)}, u32[]{:S(2)}) %collective-permute-start.18) | collective-permute-done | bytes 4128 | tf_op jit(solution)/shard_map/ppermute | solution.py:158
  114.6 7.2 %collective-permute-start.15 = (bf16[2,128,1024]{2,1,0:T(8,128)(2,1)S(1)}, bf16[2,128,1024]{2,1,0:T(8,128)(2,1)S(1)}, u32[]{:S(2)}, u32[]{:S(2)}) collective-permute-start(bf16[2,128,1024]{2,1,0:T(8,128)(2,1)S(1)} %pad_maximum_fusion), channel_id=1, source_target_pairs={{0,1},{1,0},{2,3},{3,2},{4,5},{5,4},{6,7},{7,6},{8,9},{9,8},{10,11... | collective-permute-start | bytes 1572872 | tf_op jit(solution)/shard_map/ppermute | solution.py:158
  122.2 1.3 collective-permute-start.22
  123.6 1.3 collective-permute-start.23
  125.1 1.3 collective-permute-start.27
  126.4 2.3 %collective-permute-done.22 = bf16[2,2,128,128]{3,2,1,0:T(8,128)(2,1)S(1)} collective-permute-done((bf16[2,2,128,128]{3,2,1,0:T(8,128)(2,1)S(1)}, bf16[2,2,128,128]{3,2,1,0:T(8,128)(2,1)S(1)}, u32[]{:S(2)}, u32[]{:S(2)}) %collective-permute-start.22) | collective-permute-done | bytes 131104 | tf_op jit(solution)/shard_map/ppermute | solution.py:158
  128.7 1.3 collective-permute-start.28
  130.0 1.1 collective-permute-done.23
  131.4 5.0 %collective-permute-done.28 = bf16[2,2,128,128]{3,2,1,0:T(8,128)(2,1)S(1)} collective-permute-done((bf16[2,2,128,128]{3,2,1,0:T(8,128)(2,1)S(1)}, bf16[2,2,128,128]{3,2,1,0:T(8,128)(2,1)S(1)}, u32[]{:S(2)}, u32[]{:S(2)}) %collective-permute-start.28) | collective-permute-done | bytes 131104 | tf_op jit(solution)/shard_map/ppermute | solution.py:158
  136.7 3.6 %collective-permute-start.29 = (bf16[2,2,128,128]{3,2,1,0:T(8,128)(2,1)S(1)}, bf16[2,2,128,128]{3,2,1,0:T(8,128)(2,1)S(1)}, u32[]{:S(2)}, u32[]{:S(2)}) collective-permute-start(bf16[2,2,128,128]{3,2,1,0:T(8,128)(2,1)S(1)} %slice_bitcast_fusion.4), channel_id=1, source_target_pairs={{0,1},{1,0},{2,3},{3,2},{4,5},{5,4},{6,7},{7,6},{8,9},{9,8},{10,11... | collective-permute-start | bytes 393224 | tf_op jit(solution)/shard_map/ppermute | solution.py:158
  143.5 1.2 multiply_convert_fusion
  144.9 1.1 maximum_bitcast_fusion
  (116 shorter events, 20.5 us)
Async XLA Ops:
  3.0 4.4 %collective-permute-start.2 = (bf16[2,272,128]{2,1,0:T(8,128)(2,1)S(1)}, bf16[2,272,128]{2,1,0:T(8,128)(2,1)S(1)}, u32[]{:S(2)}, u32[]{:S(2)}) collective-permute-start(bf16[2,272,128]{2,1,0:T(8,128)(2,1)S(1)} %get-tuple-element.88), channel_id=1, source_target_pairs={{0,1},{1,0},{2,3},{3,2},{4,5},{5,4},{6,7},{7,6},{8,9},{9,8},{10,11... | collective-permute-start | bytes 417800 | tf_op jit(solution)/shard_map/ppermute | solution.py:158
  5.3 33.0 %collective-permute-start = (bf16[128,2048]{1,0:T(8,128)(2,1)}, bf16[128,2048]{1,0:T(8,128)(2,1)S(1)}, u32[]{:S(2)}, u32[]{:S(2)}) collective-permute-start(bf16[128,2048]{1,0:T(8,128)(2,1)} %dynamic-slice_bitcast_fusion.1), channel_id=1, source_target_pairs={{0,1},{1,0},{2,3},{3,2},{4,5},{5,4},{6,7},{7,6},{8,9},{9,8},{10,11... | collective-permute-start | bytes 1572872 | tf_op jit(solution)/shard_map/ppermute | solution.py:158
  6.2 32.6 %collective-permute-start.1 = (bf16[128,2048]{1,0:T(8,128)(2,1)}, bf16[128,2048]{1,0:T(8,128)(2,1)S(1)}, u32[]{:S(2)}, u32[]{:S(2)}) collective-permute-start(bf16[128,2048]{1,0:T(8,128)(2,1)} %dynamic-slice_bitcast_fusion), channel_id=1, source_target_pairs={{0,1},{1,0},{2,3},{3,2},{4,5},{5,4},{6,7},{7,6},{8,9},{9,8},{10,11... | collective-permute-start | bytes 1572872 | tf_op jit(solution)/shard_map/ppermute | solution.py:158
  7.4 7.9 %collective-permute-start.3 = (bf16[2,272,128]{2,1,0:T(8,128)(2,1)S(1)}, bf16[2,272,128]{2,1,0:T(8,128)(2,1)S(1)}, u32[]{:S(2)}, u32[]{:S(2)}) collective-permute-start(bf16[2,272,128]{2,1,0:T(8,128)(2,1)S(1)} %get-tuple-element.72.own_ref), channel_id=1, source_target_pairs={{0,8},{1,9},{2,10},{3,11},{4,12},{5,13},{6,14},{7,15},{8,16},{9,17... | collective-permute-start | bytes 417800 | tf_op jit(solution)/shard_map/ppermute | solution.py:158
  9.8 9.1 %collective-permute-start.4 = (bf16[2,272,128]{2,1,0:T(8,128)(2,1)S(1)}, bf16[2,272,128]{2,1,0:T(8,128)(2,1)S(1)}, u32[]{:S(2)}, u32[]{:S(2)}) collective-permute-start(bf16[2,272,128]{2,1,0:T(8,128)(2,1)S(1)} %get-tuple-element.72.own_ref), channel_id=1, source_target_pairs={{0,16},{1,17},{2,18},{3,19},{4,20},{5,21},{6,22},{7,23},{8,24},{9,... | collective-permute-start | bytes 417800 | tf_op jit(solution)/shard_map/ppermute | solution.py:158
  15.1 12.6 %collective-permute-start.10 = (bf16[2,272,128]{2,1,0:T(8,128)(2,1)S(1)}, bf16[2,272,128]{2,1,0:T(8,128)(2,1)S(1)}, u32[]{:S(2)}, u32[]{:S(2)}) collective-permute-start(bf16[2,272,128]{2,1,0:T(8,128)(2,1)S(1)} %get-tuple-element.71.own_ref), channel_id=1, source_target_pairs={{0,8},{1,9},{2,10},{3,11},{4,12},{5,13},{6,14},{7,15},{8,16},{9,17... | collective-permute-start | bytes 417800 | tf_op jit(solution)/shard_map/ppermute | solution.py:158
  15.3 8.8 %collective-permute-start.11 = (bf16[2,272,128]{2,1,0:T(8,128)(2,1)S(1)}, bf16[2,272,128]{2,1,0:T(8,128)(2,1)S(1)}, u32[]{:S(2)}, u32[]{:S(2)}) collective-permute-start(bf16[2,272,128]{2,1,0:T(8,128)(2,1)S(1)} %get-tuple-element.71.own_ref), channel_id=1, source_target_pairs={{0,16},{1,17},{2,18},{3,19},{4,20},{5,21},{6,22},{7,23},{8,24},{9,... | collective-permute-start | bytes 417800 | tf_op jit(solution)/shard_map/ppermute | solution.py:158
  19.6 2.5 %collective-permute-start.8 = (f32[8,128]{1,0:T(8,128)S(1)}, f32[8,128]{1,0:T(8,128)S(1)}, u32[]{:S(2)}, u32[]{:S(2)}) collective-permute-start(f32[8,128]{1,0:T(8,128)S(1)} %broadcast_in_dim.33), channel_id=1, source_target_pairs={{0,32},{32,0},{64,96},{96,64},{1,33},{33,1},{65,97},{97,65},{2,34}... | collective-permute-start | bytes 12296 | tf_op jit(solution)/shard_map/ppermute | solution.py:178
  22.1 17.4 %collective-permute-start.5 = (bf16[2,2,272,128]{3,2,1,0:T(8,128)(2,1)}, bf16[2,2,272,128]{3,2,1,0:T(8,128)(2,1)S(1)}, u32[]{:S(2)}, u32[]{:S(2)}) collective-permute-start(bf16[2,2,272,128]{3,2,1,0:T(8,128)(2,1)} %get-tuple-element.83), channel_id=1, source_target_pairs={{0,2},{1,3},{2,4},{3,5},{4,6},{5,7},{6,0},{7,1},{8,10},{9,11},{10,... | collective-permute-start | bytes 835592 | tf_op jit(solution)/shard_map/ppermute | solution.py:158
  24.1 6.9 %collective-permute-start.9 = (f32[8,128]{1,0:T(8,128)S(1)}, f32[8,128]{1,0:T(8,128)S(1)}, u32[]{:S(2)}, u32[]{:S(2)}) collective-permute-start(f32[8,128]{1,0:T(8,128)S(1)} %broadcast_add_fusion), channel_id=1, source_target_pairs={{0,64},{32,96},{64,0},{96,32},{1,65},{33,97},{65,1},{97,33},{2,66}... | collective-permute-start | bytes 12296 | tf_op jit(solution)/shard_map/ppermute | solution.py:178
  27.7 13.7 %collective-permute-start.6 = (bf16[2,2,272,128]{3,2,1,0:T(8,128)(2,1)}, bf16[2,2,272,128]{3,2,1,0:T(8,128)(2,1)S(1)}, u32[]{:S(2)}, u32[]{:S(2)}) collective-permute-start(bf16[2,2,272,128]{3,2,1,0:T(8,128)(2,1)} %get-tuple-element.82), channel_id=1, source_target_pairs={{0,4},{1,5},{2,6},{3,7},{4,0},{5,1},{6,2},{7,3},{8,12},{9,13},{10,... | collective-permute-start | bytes 835592 | tf_op jit(solution)/shard_map/ppermute | solution.py:158
  31.0 11.2 %collective-permute-start.7 = (bf16[2,2,272,128]{3,2,1,0:T(8,128)(2,1)}, bf16[2,2,272,128]{3,2,1,0:T(8,128)(2,1)}, u32[]{:S(2)}, u32[]{:S(2)}) collective-permute-start(bf16[2,2,272,128]{3,2,1,0:T(8,128)(2,1)} %get-tuple-element.81), channel_id=1, source_target_pairs={{0,6},{1,7},{2,0},{3,1},{4,2},{5,3},{6,4},{7,5},{8,14},{9,15},{10,... | collective-permute-start | bytes 835592 | tf_op jit(solution)/shard_map/ppermute | solution.py:158
  38.3 37.1 %collective-permute-start.12 = (bf16[2,2,272,128]{3,2,1,0:T(8,128)(2,1)S(1)}, bf16[2,2,272,128]{3,2,1,0:T(8,128)(2,1)S(1)}, u32[]{:S(2)}, u32[]{:S(2)}) collective-permute-start(bf16[2,2,272,128]{3,2,1,0:T(8,128)(2,1)S(1)} %get-tuple-element.80), channel_id=1, source_target_pairs={{0,2},{1,3},{2,4},{3,5},{4,6},{5,7},{6,0},{7,1},{8,10},{9,11},{10,... | collective-permute-start | bytes 835592 | tf_op jit(solution)/shard_map/ppermute | solution.py:158
  38.8 36.9 %collective-permute-start.13 = (bf16[2,2,272,128]{3,2,1,0:T(8,128)(2,1)S(1)}, bf16[2,2,272,128]{3,2,1,0:T(8,128)(2,1)S(1)}, u32[]{:S(2)}, u32[]{:S(2)}) collective-permute-start(bf16[2,2,272,128]{3,2,1,0:T(8,128)(2,1)S(1)} %get-tuple-element.79), channel_id=1, source_target_pairs={{0,4},{1,5},{2,6},{3,7},{4,0},{5,1},{6,2},{7,3},{8,12},{9,13},{10,... | collective-permute-start | bytes 835592 | tf_op jit(solution)/shard_map/ppermute | solution.py:158
  39.6 36.1 %collective-permute-start.14 = (bf16[2,2,272,128]{3,2,1,0:T(8,128)(2,1)S(1)}, bf16[2,2,272,128]{3,2,1,0:T(8,128)(2,1)S(1)}, u32[]{:S(2)}, u32[]{:S(2)}) collective-permute-start(bf16[2,2,272,128]{3,2,1,0:T(8,128)(2,1)S(1)} %get-tuple-element.78), channel_id=1, source_target_pairs={{0,6},{1,7},{2,0},{3,1},{4,2},{5,3},{6,4},{7,5},{8,14},{9,15},{10,... | collective-permute-start | bytes 835592 | tf_op jit(solution)/shard_map/ppermute | solution.py:158
  69.0 44.8 %collective-permute-start.19 = (bf16[2,2,2,128,128]{4,3,2,1,0:T(8,128)(2,1)S(1)}, bf16[2,2,2,128,128]{4,3,2,1,0:T(8,128)(2,1)S(1)}, u32[]{:S(2)}, u32[]{:S(2)}) collective-permute-start(bf16[2,2,2,128,128]{4,3,2,1,0:T(8,128)(2,1)S(1)} %get-tuple-element.43), channel_id=1, source_target_pairs={{0,6},{1,7},{2,0},{3,1},{4,2},{5,3},{6,4},{7,5},{8,14},{9,15},{10,... | collective-permute-start | bytes 786440 | tf_op jit(solution)/shard_map/ppermute | solution.py:158
  72.5 42.1 %collective-permute-start.20 = (bf16[2,2,2,128,128]{4,3,2,1,0:T(8,128)(2,1)S(1)}, bf16[2,2,2,128,128]{4,3,2,1,0:T(8,128)(2,1)S(1)}, u32[]{:S(2)}, u32[]{:S(2)}) collective-permute-start(bf16[2,2,2,128,128]{4,3,2,1,0:T(8,128)(2,1)S(1)} %get-tuple-element.44), channel_id=1, source_target_pairs={{0,4},{1,5},{2,6},{3,7},{4,0},{5,1},{6,2},{7,3},{8,12},{9,13},{10,... | collective-permute-start | bytes 786440 | tf_op jit(solution)/shard_map/ppermute | solution.py:158
  75.4 46.5 %collective-permute-start.21 = (bf16[2,2,2,128,128]{4,3,2,1,0:T(8,128)(2,1)S(1)}, bf16[2,2,2,128,128]{4,3,2,1,0:T(8,128)(2,1)S(1)}, u32[]{:S(2)}, u32[]{:S(2)}) collective-permute-start(bf16[2,2,2,128,128]{4,3,2,1,0:T(8,128)(2,1)S(1)} %get-tuple-element.45), channel_id=1, source_target_pairs={{0,2},{1,3},{2,4},{3,5},{4,6},{5,7},{6,0},{7,1},{8,10},{9,11},{10,... | collective-permute-start | bytes 786440 | tf_op jit(solution)/shard_map/ppermute | solution.py:158
  102.4 19.8 %collective-permute-start.24 = (bf16[2,2,2,128,128]{4,3,2,1,0:T(8,128)(2,1)S(1)}, bf16[2,2,2,128,128]{4,3,2,1,0:T(8,128)(2,1)S(1)}, u32[]{:S(2)}, u32[]{:S(2)}) collective-permute-start(bf16[2,2,2,128,128]{4,3,2,1,0:T(8,128)(2,1)S(1)} %get-tuple-element.47), channel_id=1, source_target_pairs={{0,6},{1,7},{2,0},{3,1},{4,2},{5,3},{6,4},{7,5},{8,14},{9,15},{10,... | collective-permute-start | bytes 786440 | tf_op jit(solution)/shard_map/ppermute | solution.py:158
  105.1 3.6 %collective-permute-start.17 = (f32[8,128]{1,0:T(8,128)S(1)}, f32[8,128]{1,0:T(8,128)S(1)}, u32[]{:S(2)}, u32[]{:S(2)}) collective-permute-start(f32[8,128]{1,0:T(8,128)S(1)} %get-tuple-element.41), channel_id=1, source_target_pairs={{0,8},{1,9},{2,10},{3,11},{4,12},{5,13},{6,14},{7,15},{8,0},{9,1},... | collective-permute-start | bytes 12296 | tf_op jit(solution)/shard_map/ppermute | solution.py:158
  107.7 6.9 %copy-start.7 = (f32[2]{0:T(128)S(1)}, f32[2]{0:T(128)}, u32[]{:S(2)}) copy-start(f32[2]{0:T(128)} %constant.106.clone) | copy-start | bytes 28
  107.7 6.8 %copy-start.1 = (bf16[128,2048]{1,0:T(8,128)(2,1)}, bf16[128,2048]{1,0:T(8,128)(2,1)S(1)}, u32[]{:S(2)}) copy-start(bf16[128,2048]{1,0:T(8,128)(2,1)S(1)} %constant_dynamic-update-slice_fusion.2) | copy-start | bytes 1572868
  108.7 4.0 %collective-permute-start.18 = (f32[8,128]{1,0:T(8,128)S(1)}, f32[8,128]{1,0:T(8,128)S(1)}, u32[]{:S(2)}, u32[]{:S(2)}) collective-permute-start(f32[8,128]{1,0:T(8,128)S(1)} %add.161), channel_id=1, source_target_pairs={{0,16},{1,17},{2,18},{3,19},{4,20},{5,21},{6,22},{7,23},{8,24},{9,... | collective-permute-start | bytes 12296 | tf_op jit(solution)/shard_map/ppermute | solution.py:158
  112.6 10.9 %collective-permute-start.25 = (bf16[2,2,2,128,128]{4,3,2,1,0:T(8,128)(2,1)S(1)}, bf16[2,2,2,128,128]{4,3,2,1,0:T(8,128)(2,1)S(1)}, u32[]{:S(2)}, u32[]{:S(2)}) collective-permute-start(bf16[2,2,2,128,128]{4,3,2,1,0:T(8,128)(2,1)S(1)} %get-tuple-element.48), channel_id=1, source_target_pairs={{0,4},{1,5},{2,6},{3,7},{4,0},{5,1},{6,2},{7,3},{8,12},{9,13},{10,... | collective-permute-start | bytes 786440 | tf_op jit(solution)/shard_map/ppermute | solution.py:158
  113.8 11.1 %collective-permute-start.26 = (bf16[2,2,2,128,128]{4,3,2,1,0:T(8,128)(2,1)S(1)}, bf16[2,2,2,128,128]{4,3,2,1,0:T(8,128)(2,1)S(1)}, u32[]{:S(2)}, u32[]{:S(2)}) collective-permute-start(bf16[2,2,2,128,128]{4,3,2,1,0:T(8,128)(2,1)S(1)} %get-tuple-element.49), channel_id=1, source_target_pairs={{0,2},{1,3},{2,4},{3,5},{4,6},{5,7},{6,0},{7,1},{8,10},{9,11},{10,... | collective-permute-start | bytes 786440 | tf_op jit(solution)/shard_map/ppermute | solution.py:158
  114.6 25.6 %collective-permute-start.15 = (bf16[2,128,1024]{2,1,0:T(8,128)(2,1)S(1)}, bf16[2,128,1024]{2,1,0:T(8,128)(2,1)S(1)}, u32[]{:S(2)}, u32[]{:S(2)}) collective-permute-start(bf16[2,128,1024]{2,1,0:T(8,128)(2,1)S(1)} %pad_maximum_fusion), channel_id=1, source_target_pairs={{0,1},{1,0},{2,3},{3,2},{4,5},{5,4},{6,7},{7,6},{8,9},{9,8},{10,11... | collective-permute-start | bytes 1572872 | tf_op jit(solution)/shard_map/ppermute | solution.py:158
  121.9 21.3 %collective-permute-start.16 = (bf16[2,128,1024]{2,1,0:T(8,128)(2,1)S(1)}, bf16[2,128,1024]{2,1,0:T(8,128)(2,1)S(1)}, u32[]{:S(2)}, u32[]{:S(2)}) collective-permute-start(bf16[2,128,1024]{2,1,0:T(8,128)(2,1)S(1)} %pad_maximum_fusion.1), channel_id=1, source_target_pairs={{0,1},{1,0},{2,3},{3,2},{4,5},{5,4},{6,7},{7,6},{8,9},{9,8},{10,11... | collective-permute-start | bytes 1572872 | tf_op jit(solution)/shard_map/ppermute | solution.py:158
  122.2 6.5 %collective-permute-start.22 = (bf16[2,2,128,128]{3,2,1,0:T(8,128)(2,1)S(1)}, bf16[2,2,128,128]{3,2,1,0:T(8,128)(2,1)S(1)}, u32[]{:S(2)}, u32[]{:S(2)}) collective-permute-start(bf16[2,2,128,128]{3,2,1,0:T(8,128)(2,1)S(1)} %get-tuple-element.54), channel_id=1, source_target_pairs={{8,0},{9,1},{10,2},{11,3},{12,4},{13,5},{14,6},{15,7},{16,8},{17,9... | collective-permute-start | bytes 393224 | tf_op jit(solution)/shard_map/ppermute | solution.py:158
  123.6 7.5 %collective-permute-start.23 = (bf16[2,2,128,128]{3,2,1,0:T(8,128)(2,1)S(1)}, bf16[2,2,128,128]{3,2,1,0:T(8,128)(2,1)S(1)}, u32[]{:S(2)}, u32[]{:S(2)}) collective-permute-start(bf16[2,2,128,128]{3,2,1,0:T(8,128)(2,1)S(1)} %get-tuple-element.55), channel_id=1, source_target_pairs={{16,0},{17,1},{18,2},{19,3},{20,4},{21,5},{22,6},{23,7},{24,8},{25... | collective-permute-start | bytes 393224 | tf_op jit(solution)/shard_map/ppermute | solution.py:158
  125.1 6.3 %collective-permute-start.27 = (bf16[2,2,128,128]{3,2,1,0:T(8,128)(2,1)S(1)}, bf16[2,2,128,128]{3,2,1,0:T(8,128)(2,1)S(1)}, u32[]{:S(2)}, u32[]{:S(2)}) collective-permute-start(bf16[2,2,128,128]{3,2,1,0:T(8,128)(2,1)S(1)} %get-tuple-element.56), channel_id=1, source_target_pairs={{8,0},{9,1},{10,2},{11,3},{12,4},{13,5},{14,6},{15,7},{16,8},{17,9... | collective-permute-start | bytes 393224 | tf_op jit(solution)/shard_map/ppermute | solution.py:158
  128.7 7.8 %collective-permute-start.28 = (bf16[2,2,128,128]{3,2,1,0:T(8,128)(2,1)S(1)}, bf16[2,2,128,128]{3,2,1,0:T(8,128)(2,1)S(1)}, u32[]{:S(2)}, u32[]{:S(2)}) collective-permute-start(bf16[2,2,128,128]{3,2,1,0:T(8,128)(2,1)S(1)} %get-tuple-element.57), channel_id=1, source_target_pairs={{16,0},{17,1},{18,2},{19,3},{20,4},{21,5},{22,6},{23,7},{24,8},{25... | collective-permute-start | bytes 393224 | tf_op jit(solution)/shard_map/ppermute | solution.py:158
  136.7 4.6 %collective-permute-start.29 = (bf16[2,2,128,128]{3,2,1,0:T(8,128)(2,1)S(1)}, bf16[2,2,128,128]{3,2,1,0:T(8,128)(2,1)S(1)}, u32[]{:S(2)}, u32[]{:S(2)}) collective-permute-start(bf16[2,2,128,128]{3,2,1,0:T(8,128)(2,1)S(1)} %slice_bitcast_fusion.4), channel_id=1, source_target_pairs={{0,1},{1,0},{2,3},{3,2},{4,5},{5,4},{6,7},{7,6},{8,9},{9,8},{10,11... | collective-permute-start | bytes 393224 | tf_op jit(solution)/shard_map/ppermute | solution.py:158
  (6 other events, 15.2 us)
